TPU v7x, 32 devices: a whole 2x2x4 slice. The times are simulated.
32 devices in a mesh: seq: 4 (over y, core), exp: 8 (over z, x).
Axes of the slice: x: 2, y: 2, z: 4, core: 2. Of those that a mesh axis runs over, the one named last changes fastest.
Arguments:
- resid: bfloat16 [8, 512, 4096], P('exp', 'seq'), may hold values from -1.5 to 1.5
- queries: bfloat16 [8, 512, 4096], P('exp', 'seq'), may hold values from -8 to 8
- span_rotated_keys: bfloat16 [8, 512, 512], P('exp', 'seq'), may hold values from -6 to 6
- span_value_rows: bfloat16 [8, 512, 512], P('exp', 'seq'), may hold values from -6 to 6
- key_cache: bfloat16 [8, 4, 256, 128], P('exp', None, 'seq'), may hold values from -8 to 8
- prefix_value_cache: bfloat16 [8, 4, 256, 128], P('exp', None, 'seq'), may hold values from -6 to 6
- prefix_len: int32 [8], P('exp'), may hold values from 1 to 256, as said below
- out_weight: bfloat16 [4096, 4096], P('seq'), may hold values from -0.09375 to 0.09375
- norm_gain: float32 [4096], replicated, may hold values from 0.1 to 1.9
- router_weight: bfloat16 [4096, 32], replicated
- expert_ids: int32 [8, 512, 8], P('exp', 'seq'), may hold values from 0 to 31, all different within a row; in each aligned block of 128 rows (0 to 127, 128 to 255, ..., all dimensions but the last counted through in order) at most 36 rows name the same one
- w_gate: bfloat16 [32, 4096, 768], P(('seq', 'exp')), may hold values from -0.09375 to 0.09375
- w_up: bfloat16 [32, 4096, 768], P(('seq', 'exp')), may hold values from -0.09375 to 0.09375
- w_down: bfloat16 [32, 768, 4096], P(('seq', 'exp')), may hold values from -0.21875 to 0.21875
Outputs:
- layer_out: bfloat16 [8, 512, 4096], P('exp', 'seq')
Inputs may be any that keep to these rules, and one draw needn't show every extreme that they name: `expert_ids`: in the 128 consecutive tokens of one index of seq, no expert is named by more than 36 routes, a bound that some block reaches. `prefix_len`: some prompt's prefix fills the cache.
All inputs are finite; a program needn't handle non-finite values.
Results may differ from a plain program's by a relative error of at most 0.03.
Values may be sent and summed in bfloat16 or wider, within the bound.
A program may use at most 192 MiB of HBM per device.

v0:
```python
import jax
import jax.numpy as jnp
import numpy as np
from jax import lax
from jax.sharding import PartitionSpec as P

QUERY_HEAD_HALF = 32
KEY_VALUE_HEADS = 4
HEAD_SIZE = 128
TOP = 8


def expert_mlp(token_rows, gate_part, up_part, down_part):
    gate_val = jnp.dot(token_rows, gate_part, preferred_element_type=jnp.float32)
    up_val = jnp.dot(token_rows, up_part, preferred_element_type=jnp.float32)
    activated = (jax.nn.silu(gate_val) * up_val).astype(jnp.bfloat16)
    return jnp.dot(activated, down_part, preferred_element_type=jnp.float32).astype(jnp.bfloat16)


def per_device(
    resid,
    queries,
    span_rotated_keys,
    span_value_rows,
    key_cache,
    prefix_value_cache,
    prefix_len,
    out_weight,
    norm_gain,
    router_weight,
    expert_ids,
    w_gate,
    w_up,
    w_down,
):
    seq_count = lax.axis_size("seq")
    exp_count = lax.axis_size("exp")
    token_row_block = queries.shape[1]
    model_width = resid.shape[2]
    heads_here = QUERY_HEAD_HALF // seq_count
    group_length = QUERY_HEAD_HALF // KEY_VALUE_HEADS
    key_value_choice = np.arange(seq_count) * heads_here // group_length
    query_parts = queries[0].reshape(token_row_block, seq_count, heads_here * HEAD_SIZE)
    newest_keys = span_rotated_keys[0].reshape(token_row_block, KEY_VALUE_HEADS, HEAD_SIZE)[
        :, key_value_choice, :
    ]
    newest_values = span_value_rows[0].reshape(token_row_block, KEY_VALUE_HEADS, HEAD_SIZE)[
        :, key_value_choice, :
    ]
    fresh_pairs = jnp.concatenate([newest_keys, newest_values], axis=2)
    query_heads, span_pairs = (
        lax.all_to_all(query_parts, "seq", split_axis=1, concat_axis=0, tiled=True),
        lax.all_to_all(fresh_pairs, "seq", split_axis=1, concat_axis=0, tiled=True),
    )
    cache_pairs = jnp.concatenate(
        [key_cache[0][key_value_choice], prefix_value_cache[0][key_value_choice]], axis=2
    )
    prefix_pairs = lax.all_to_all(cache_pairs, "seq", split_axis=0, concat_axis=1, tiled=True)[0]
    span_length = query_heads.shape[0]
    prefix_total = prefix_pairs.shape[0]
    all_keys = jnp.concatenate([prefix_pairs[:, :HEAD_SIZE], span_pairs[:, 0, :HEAD_SIZE]], axis=0)
    all_values = jnp.concatenate(
        [prefix_pairs[:, HEAD_SIZE:], span_pairs[:, 0, HEAD_SIZE:]], axis=0
    )
    query_block = query_heads.reshape(span_length, heads_here, HEAD_SIZE)
    scores = jnp.einsum(
        "thd,jd->htj", query_block, all_keys, preferred_element_type=jnp.float32
    ) * HEAD_SIZE ** (-0.5)
    position = jnp.arange(prefix_total + span_length, dtype=jnp.int32)
    query_pos = jnp.arange(span_length, dtype=jnp.int32)
    usable_keys = jnp.where(
        position[None, :] < prefix_total,
        position[None, :] < prefix_len[0],
        position[None, :] - prefix_total <= query_pos[:, None],
    )
    scores = jnp.where(usable_keys[None], scores, -1e30)
    top_score = jnp.max(scores, axis=2, keepdims=True)
    raised = jnp.exp(scores - top_score)
    attn_weights = (raised / jnp.sum(raised, axis=2, keepdims=True)).astype(jnp.bfloat16)
    attended = jnp.einsum(
        "htj,jd->thd", attn_weights, all_values, preferred_element_type=jnp.float32
    ).astype(jnp.bfloat16)
    attended = attended.reshape(span_length, heads_here * HEAD_SIZE)
    projected = lax.psum_scatter(
        jnp.dot(attended, out_weight, preferred_element_type=jnp.float32).astype(jnp.bfloat16),
        "seq",
        scatter_dimension=0,
        tiled=True,
    ).astype(jnp.float32)
    hidden_state = resid[0].astype(jnp.float32) + projected
    mean_square = jnp.mean(hidden_state * hidden_state, axis=1, keepdims=True)
    normed = (hidden_state * lax.rsqrt(mean_square + 1e-06) * norm_gain).astype(jnp.bfloat16)
    logits = jnp.dot(normed, router_weight, preferred_element_type=jnp.float32)
    chosen_ids = expert_ids[0]
    chosen = jnp.take_along_axis(logits, chosen_ids, axis=1)
    route_weight = jax.nn.softmax(chosen, axis=1)
    expert_total = seq_count * exp_count
    capacity = max(2, (token_row_block * TOP * 9 + 8 * expert_total - 1) // (8 * expert_total))
    flat_ids = chosen_ids.reshape(-1)
    one_hot = (flat_ids[:, None] == jnp.arange(expert_total, dtype=jnp.int32)[None, :]).astype(
        jnp.int32
    )
    running_rank = jnp.cumsum(one_hot, axis=0) - 1
    slot_index = jnp.sum(one_hot * running_rank, axis=1)
    target = flat_ids * capacity + slot_index
    source_token = jnp.arange(token_row_block * TOP, dtype=jnp.int32) // TOP
    slot_token = (
        jnp.full((expert_total * capacity,), token_row_block, jnp.int32)
        .at[target]
        .set(source_token)
    )
    padded = jnp.concatenate([normed, jnp.zeros((1, model_width), jnp.bfloat16)], axis=0)
    send_rows = padded[slot_token].reshape(expert_total, capacity, model_width)
    gate_part = w_gate[0]
    up_part = w_up[0]
    down_part = w_down[0]
    received = lax.all_to_all(send_rows, ("seq", "exp"), split_axis=0, concat_axis=0, tiled=True)
    flat_rows = received.reshape(-1, model_width)
    returned = lax.all_to_all(
        expert_mlp(flat_rows, gate_part, up_part, down_part).reshape(received.shape),
        ("seq", "exp"),
        split_axis=0,
        concat_axis=0,
        tiled=True,
    )
    route_rows = (
        returned.reshape(-1, model_width)[target]
        .astype(jnp.float32)
        .reshape(token_row_block, TOP, model_width)
    )
    mixture = jnp.sum(route_weight[:, :, None] * route_rows, axis=1)
    return (hidden_state + mixture).astype(jnp.bfloat16)[None]


def solution(mesh):
    in_specs = (
        P("exp", "seq", None),
        P("exp", "seq", None),
        P("exp", "seq", None),
        P("exp", "seq", None),
        P("exp", None, "seq", None),
        P("exp", None, "seq", None),
        P("exp"),
        P("seq", None),
        P(),
        P(),
        P("exp", "seq", None),
        P(("seq", "exp"), None, None),
        P(("seq", "exp"), None, None),
        P(("seq", "exp"), None, None),
    )
    out_specs = P("exp", "seq", None)
    return jax.shard_map(
        per_device, mesh=mesh, in_specs=in_specs, out_specs=out_specs, check_vma=False
    )
```

profile of v0, /device:TPU:0, one launch (start us, length us, event | category | flops | bytes accessed | tf_op | source)
XLA Modules:
  0.0 724.2 jit_solution(3442284542632990199)
XLA Ops:
  6.5 1.4 gather_fusion.1
  8.0 1.4 gather_fusion
  10.1 4.2 all-to-all-start
  18.9 3.4 all-to-all-start.1
  23.0 1.9 reshape_squeeze.12
  24.9 1.3 copy.38
  26.2 2.2 all-to-all-done.1
  28.4 3.5 all-to-all-start.2
  32.8 13.6 %all-to-all-done.2 = bf16[128,4,1024]{2,0,1:T(8,128)(2,1)S(1)} async-done(((bf16[128,4,1024]{2,0,1:T(8,128)(2,1)}), bf16[128,4,1024]{2,0,1:T(8,128)(2,1)S(1)}, u32[]{:S(2)}, u32[]{:S(2)}) %all-to-all-start.2) | async-done | bytes 1048608 | tf_op jit(solution)/shard_map/all_to_all | solution.py:52
  46.6 7.3 %fusion.54 = (f32[8,512]{1,0:T(8,128)S(1)}, f32[8,512,768]{1,2,0:T(8,128)}) fusion(pred[512,768]{0,1:T(8,128)(4,1)S(1)} %fusion.18, bf16[512,8,128]{2,1,0:T(8,128)(2,1)S(1)} %bitcast.115, bf16[512,128]{1,0:T(8,128)(2,1)S(1)} %get-tuple-element.6, bf16[256,128]{1,0:T(8,128)(2,1)S(1)} %get-tuple-element.8), kind=kOutput, calls=%fused_computation.90 | convolution fusion | flops 818283264 | bytes 14237696 | tf_op jit(solution)/shard_map/sub | solution.py:78
  53.9 5.6 fusion.19
  59.5 9.5 %convolution_convert_fusion.1 = bf16[512,4096]{1,0:T(8,128)(2,1)} fusion(bf16[512,1024]{0,1:T(8,128)(2,1)S(1)} %bitcast.131, bf16[1024,4096]{1,0:T(8,128)(2,1)} %param.26), kind=kOutput, calls=%fused_computation.25 | convolution fusion | flops 4297064448 | bytes 13631488 | tf_op jit(solution)/shard_map/dot_general | solution.py:85
  69.5 9.0 %reduce-window.6 = s32[32,8,128]{2,1,0:T(8,128)S(1)} reduce-window(s32[32,8,128]{2,1,0:T(8,128)S(1)} %fusion.34, s32[]{:T(128)} %constant.63.clone.1), window={size=1x1x128 pad=0_0x0_0x127_0}, to_apply=%region_6.7 | reduce-window | flops 4161536 | bytes 262148 | tf_op jit(solution)/shard_map/reduce-window
  79.1 4.3 scatter_custom_fusion
  83.4 31.2 %reduce-scatter.2.cloned.1.call-done = bf16[128,4096]{1,0:T(8,128)(2,1)} async-done(((bf16[512,4096]{1,0:T(8,128)(2,1)}), bf16[128,4096]{1,0:T(8,128)(2,1)}) %reduce-scatter.2.cloned.1.call-update) | async-done | bytes 1048592 | tf_op jit(solution)/shard_map/reduce_scatter | solution.py:84
  114.6 1.6 multiply_reduce_fusion
  116.3 1.6 multiply_convert_fusion
  118.0 7.9 %gather_fusion.4 = bf16[1152,4096]{1,0:T(8,128)(2,1)} fusion(bf16[129,4096]{1,0:T(8,128)(2,1)S(1)} %concatenate.19, s32[2048]{0:T(1024)S(1)} %pad_clamp_fusion), kind=kCustom, calls=%fused_computation.4 | custom fusion | bytes 18878976 | tf_op jit(solution)/shard_map/gather | solution.py:113
  125.9 13.2 %reshape.236 = bf16[32,36,4096]{2,1,0:T(8,128)(2,1)} reshape(bf16[1152,4096]{1,0:T(8,128)(2,1)} %gather_fusion.4) | data formatting | bytes 18874368 | tf_op jit(solution)/shard_map/reshape | solution.py:113
  139.1 234.6 %all_to_all.52 = bf16[32,36,4096]{2,1,0:T(8,128)(2,1)} all-to-all(bf16[32,36,4096]{2,1,0:T(8,128)(2,1)} %reshape.236), channel_id=1, replica_groups=mesh['seq'=4,'exp'=8] {'seq','exp'}, dimensions={0} | all-to-all | bytes 18874368 | tf_op jit(solution)/shard_map/all_to_all | solution.py:117
  373.6 13.3 %reshape.237 = bf16[1152,4096]{1,0:T(8,128)(2,1)} reshape(bf16[32,36,4096]{2,1,0:T(8,128)(2,1)} %all_to_all.52) | data formatting | bytes 18874368 | tf_op jit(solution)/shard_map/reshape | solution.py:118
  386.9 12.0 %fusion.6 = f32[1152,768]{1,0:T(8,128)S(1)} fusion(bf16[1152,4096]{1,0:T(8,128)(2,1)} %reshape.237, bf16[1,4096,768]{2,1,0:T(8,128)(2,1)} %param.30), kind=kOutput, calls=%fused_computation.19 | convolution fusion | flops 7247757312 | bytes 19267584 | tf_op jit(solution)/shard_map/dot_general | solution.py:14
  398.9 10.3 %fusion.15 = bf16[1152,768]{1,0:T(8,128)(2,1)S(1)} fusion(bf16[1152,4096]{1,0:T(8,128)(2,1)S(1)} %copy-done.3, bf16[1,4096,768]{2,1,0:T(8,128)(2,1)} %param.31, f32[1152,768]{1,0:T(8,128)S(1)} %fusion.6), kind=kOutput, calls=%fused_computation.27 | convolution fusion | flops 7253065728 | bytes 21037056 | tf_op jit(solution)/shard_map/dot_general | solution.py:15
  409.3 9.6 %convolution_convert_fusion = bf16[1152,4096]{1,0:T(8,128)(2,1)} fusion(bf16[1152,768]{1,0:T(8,128)(2,1)S(1)} %fusion.15, bf16[1,768,4096]{2,1,0:T(8,128)(2,1)S(1)} %bitcast.130), kind=kOutput, calls=%fused_computation.11 | convolution fusion | flops 7252475904 | bytes 17498112 | tf_op jit(solution)/shard_map/dot_general | solution.py:17
  418.8 13.1 %reshape.238 = bf16[32,36,4096]{2,1,0:T(8,128)(2,1)} reshape(bf16[1152,4096]{1,0:T(8,128)(2,1)} %convolution_convert_fusion) | data formatting | bytes 18874368 | tf_op jit(solution)/shard_map/reshape | solution.py:120
  432.0 3.7 all-to-all-start.4
  436.3 7.0 gather_fusion.6
  443.9 224.0 %all-to-all-done.4 = bf16[32,36,4096]{2,1,0:T(8,128)(2,1)} async-done(((bf16[32,36,4096]{2,1,0:T(8,128)(2,1)}), bf16[32,36,4096]{2,1,0:T(8,128)(2,1)}, u32[]{:S(2)}, u32[]{:S(2)}) %all-to-all-start.4) | async-done | bytes 9437216 | tf_op jit(solution)/shard_map/all_to_all | solution.py:119
  667.9 13.2 %reshape.239 = bf16[1152,4096]{1,0:T(8,128)(2,1)} reshape(bf16[32,36,4096]{2,1,0:T(8,128)(2,1)} %all-to-all-done.4) | data formatting | bytes 18874368 | tf_op jit(solution)/shard_map/reshape | solution.py:127
  681.2 20.0 %gather_fusion.5 = bf16[1024,4096]{1,0:T(8,128)(2,1)} fusion(bf16[1152,4096]{1,0:T(8,128)(2,1)} %reshape.239, s32[1024]{0:T(1024)S(1)} %broadcast_clamp_fusion), kind=kCustom, calls=%fused_computation.5 | custom fusion | bytes 16781312 | tf_op jit(solution)/shard_map/gather | solution.py:127
  701.1 13.3 %fusion.1 = f32[128,4096]{1,0:T(8,128)} fusion(bf16[1024,4096]{1,0:T(8,128)(2,1)} %gather_fusion.5, f32[128,8]{1,0:T(8,128)S(1)} %fusion.35), kind=kLoop, calls=%fused_computation.10 | loop fusion | flops 12058624 | bytes 10489856 | tf_op jit(solution)/shard_map/reduce_sum | solution.py:131
  714.4 2.9 fusion.22
  (65 shorter events, 8.7 us)
Async XLA Ops:
  6.5 429.4 %copy-start = (bf16[4096,32]{0,1:T(8,128)(2,1)S(1)}, bf16[4096,32]{0,1:T(8,128)(2,1)}, u32[]{:S(2)}) copy-start(bf16[4096,32]{0,1:T(8,128)(2,1)} %param.28) | copy-start | bytes 786436
  10.1 8.9 %all-to-all-start = ((bf16[4,64,256]{2,1,0:T(8,128)(2,1)}), bf16[4,64,256]{2,1,0:T(8,128)(2,1)S(1)}, u32[]{:S(2)}, u32[]{:S(2)}) async-start(bf16[4,64,256]{2,1,0:T(8,128)(2,1)} %pad_maximum_fusion.1), calls=%async_computation | async-start | bytes 262144 | tf_op jit(solution)/shard_map/all_to_all | solution.py:58
  18.9 9.4 %all-to-all-start.1 = ((bf16[128,4,256]{2,0,1:T(8,128)(2,1)}), bf16[128,4,256]{2,0,1:T(8,128)(2,1)S(1)}, u32[]{:S(2)}, u32[]{:S(2)}) async-start(bf16[128,4,256]{2,0,1:T(8,128)(2,1)} %pad_maximum_fusion), calls=%async_computation.1 | async-start | bytes 524288 | tf_op jit(solution)/shard_map/all_to_all | solution.py:53
  28.4 18.0 %all-to-all-start.2 = ((bf16[128,4,1024]{2,0,1:T(8,128)(2,1)}), bf16[128,4,1024]{2,0,1:T(8,128)(2,1)S(1)}, u32[]{:S(2)}, u32[]{:S(2)}) async-start(bf16[128,4,1024]{2,0,1:T(8,128)(2,1)} %copy.38), calls=%async_computation.2 | async-start | bytes 2097152 | tf_op jit(solution)/shard_map/all_to_all | solution.py:52
  31.9 82.7 %reduce-scatter.2.cloned.1.call-start = ((), (), s32[]{:S(2)}) async-start(), calls=%async_computation.6 | async-start | bytes 5242880 | tf_op jit(solution)/shard_map/reduce_scatter | solution.py:84
  59.5 9.5 %copy-start.4 = (s32[1,128,8]{1,2,0:T(8,128)S(1)}, s32[1,128,8]{1,2,0:T(8,128)}, u32[]{:S(2)}) copy-start(s32[1,128,8]{1,2,0:T(8,128)} %param.29) | copy-start | bytes 12292
  69.0 45.6 %copy-start.1 = (bf16[1,128,4096]{2,1,0:T(8,128)(2,1)S(1)}, bf16[1,128,4096]{2,1,0:T(8,128)(2,1)}, u32[]{:S(2)}) copy-start(bf16[1,128,4096]{2,1,0:T(8,128)(2,1)} %param.19) | copy-start | bytes 3145732
  69.0 47.3 %copy-start.5 = (f32[4096]{0:T(1024)S(1)}, f32[4096]{0:T(1024)}, u32[]{:S(2)}) copy-start(f32[4096]{0:T(1024)} %param.27) | copy-start | bytes 49156
  386.9 12.0 %copy-start.3 = (bf16[1152,4096]{1,0:T(8,128)(2,1)S(1)}, bf16[1152,4096]{1,0:T(8,128)(2,1)}, u32[]{:S(2)}) copy-start(bf16[1152,4096]{1,0:T(8,128)(2,1)} %reshape.237) | copy-start | bytes 28311556
  386.9 22.3 %slice-start = ((s8[6291456]{0:T(1024)(128)(4,1)}), s8[4194304]{0:T(1024)(128)(4,1)S(1)}, s32[]{:S(2)}) async-start(s8[6291456]{0:T(1024)(128)(4,1)} %bitcast.129), calls=%async_computation.7 | async-start | bytes 8388608
  398.9 10.3 %slice-start.1 = ((s8[6291456]{0:T(1024)(128)(4,1)}), s8[2097152]{0:T(1024)(128)(4,1)S(1)}, s32[]{:S(2)}) async-start(s8[6291456]{0:T(1024)(128)(4,1)} %bitcast.129), calls=%async_computation.8 | async-start | bytes 4194304
  432.0 236.0 %all-to-all-start.4 = ((bf16[32,36,4096]{2,1,0:T(8,128)(2,1)}), bf16[32,36,4096]{2,1,0:T(8,128)(2,1)}, u32[]{:S(2)}, u32[]{:S(2)}) async-start(bf16[32,36,4096]{2,1,0:T(8,128)(2,1)} %reshape.238), calls=%async_computation.5 | async-start | bytes 20971520 | tf_op jit(solution)/shard_map/all_to_all | solution.py:119
  701.1 13.3 %copy-start.2 = (bf16[128,4096]{1,0:T(8,128)(2,1)S(1)}, bf16[128,4096]{1,0:T(8,128)(2,1)}, u32[]{:S(2)}) copy-start(bf16[128,4096]{1,0:T(8,128)(2,1)} %reduce-scatter.2.cloned.1.call-done) | copy-start | bytes 3145732
Sparse Core Ops, SparseCore 0:
  69.1 45.4 reduce-scatter.1
where the time goes:
time: 729 us; the launch traced here: 724 us
  waiting for transfers between devices  271 us (37%)
  blocking collectives  235 us (32%)
  local copies, waits for them, and re-layouts  103 us (14%)
  matrix products  54.7 us (8%)
  other arithmetic  31.3 us (4%)
  starting transfers between devices  14.9 us (2%)
  between operations  14.4 us (2%)
    all_to_all x1, blocking collectives, per_device(): lax.all_to_all(send_rows, ('seq', 'exp'), split_axis=0, concat_axis=0, ti...  235 us
    all_to_all x1, waiting for transfers between devices, per_device(): lax.all_to_all(expert_mlp(flat_rows, gate_part, up_part, down_part).resha...  224 us
    reduce_scatter x1, waiting for transfers between devices, per_device(): lax.psum_scatter(jnp.dot(attended, out_weight, preferred_element_type=jnp...  31.2 us
    gather x1, local copies, waits for them, and re-layouts, per_device(): returned.reshape(-1, model_width)[target].astype(jnp.float32)  20 us
  transfers between devices with their start and end apart: 5, of which 5 were waited for; matrix products, arithmetic and copies ran while one was open for 4% of the time, Pallas kernels for 0%

commit v1 on v0

--- a/solution.py
+++ b/solution.py
@@ -1,7 +1,11 @@
+import functools
+
 import jax
 import jax.numpy as jnp
 import numpy as np
 from jax import lax
+from jax.experimental import pallas as pl
+from jax.experimental.pallas import tpu as pltpu
 from jax.sharding import PartitionSpec as P
 
 QUERY_HEAD_HALF = 32
@@ -10,11 +14,367 @@
 TOP = 8
 
 
-def expert_mlp(token_rows, gate_part, up_part, down_part):
-    gate_val = jnp.dot(token_rows, gate_part, preferred_element_type=jnp.float32)
-    up_val = jnp.dot(token_rows, up_part, preferred_element_type=jnp.float32)
-    activated = (jax.nn.silu(gate_val) * up_val).astype(jnp.bfloat16)
-    return jnp.dot(activated, down_part, preferred_element_type=jnp.float32).astype(jnp.bfloat16)
+LINE = 4
+MESH = pl.DeviceIdType.MESH
+VMEM_BYTES = 60 * 1024 * 1024
+
+
+class Place:
+    def __init__(self, line, width, seq_count):
+        self.line, self.width, self.plane = line, width, width * seq_count
+        self.seq, exp = lax.axis_index("seq"), lax.axis_index("exp")
+        self.z, self.x = lax.div(exp, width), lax.rem(exp, width)
+        self.me = self.seq * width + self.x
+
+    def on_line(self, k):
+        z = lax.rem(self.z + k, self.line)
+        return z, {"seq": self.seq, "exp": z * self.width + self.x}
+
+    def in_plane(self, k):
+        j = lax.rem(self.me + k, self.plane)
+        return j, {
+            "seq": lax.div(j, self.width),
+            "exp": self.z * self.width + lax.rem(j, self.width),
+        }
+
+    def greet(self):
+        barrier = pltpu.get_barrier_semaphore()
+        for k in range(1, self.line):
+            pl.semaphore_signal(
+                barrier, inc=1, device_id=self.on_line(k)[1], device_id_type=MESH
+            )
+        for k in range(1, self.plane):
+            pl.semaphore_signal(
+                barrier, inc=1, device_id=self.in_plane(k)[1], device_id_type=MESH
+            )
+        pl.semaphore_wait(barrier, self.line + self.plane - 2)
+
+
+def span(start, size, step):
+    return pl.ds(pl.multiple_of(start * size, step), size)
+
+
+def remote(src, dst, send, recv, target):
+    return pltpu.make_async_remote_copy(
+        src_ref=src, dst_ref=dst, send_sem=send, recv_sem=recv,
+        device_id=target, device_id_type=MESH,
+    )
+
+
+def dispatch_kernel(
+    line, width, seq_count, cap,
+    normed_ref, pick_ref, router_ref, gate_hbm, up_hbm,
+    act_ref, logit_ref,
+    lines, pack, rows_in, gate, up, gate_sum, up_sum,
+    line_send, line_recv, plane_send, plane_recv, weight_sem,
+):
+    at = Place(line, width, seq_count)
+    chunks, _, cw = lines.shape
+    tokens = normed_ref.shape[0]
+    plane = at.plane
+    total = plane * cap
+    block = total // 4
+
+    def weight_copies(c):
+        return (
+            pltpu.make_async_copy(gate_hbm.at[span(c, cw, cw)], gate.at[c], weight_sem.at[0, c]),
+            pltpu.make_async_copy(up_hbm.at[span(c, cw, cw)], up.at[c], weight_sem.at[1, c]),
+        )
+
+    def start_weights(c, carry):
+        for copy in weight_copies(c):
+            copy.start()
+        return carry
+
+    lax.fori_loop(0, chunks, start_weights, 0)
+    own = span(at.z, tokens, tokens)
+    for c in range(chunks):
+        lines[c, own, :] = normed_ref[:, c * cw : (c + 1) * cw]
+    gate_sum[...] = jnp.zeros_like(gate_sum)
+    up_sum[...] = jnp.zeros_like(up_sum)
+    logit_ref[...] = jnp.zeros_like(logit_ref)
+    at.greet()
+
+    def line_start(c):
+        for k in range(1, line):
+            target = at.on_line(k)[1]
+            part = lines.at[c, own]
+            remote(part, part, line_send.at[c], line_recv.at[c], target).start()
+
+    def line_bulk(c):
+        part = lines.at[c, pl.ds(0, (line - 1) * tokens)]
+        return remote(part, part, line_send.at[c], line_recv.at[c], at.on_line(1)[1])
+
+    def plane_bulk(c):
+        part = pl.ds(0, (plane - 1) * cap)
+        return remote(
+            pack.at[lax.rem(c, 2), part], rows_in.at[c, part],
+            plane_send.at[c], plane_recv.at[c], at.in_plane(1)[1],
+        )
+
+    def plane_start(c):
+        slot = lax.rem(c, 2)
+
+        @pl.when(c >= 2)
+        def _():
+            plane_bulk(c - 2).wait_send()
+
+        for b in range(4):
+            part = pl.ds(b * block, block)
+            pack[slot, part, :] = jnp.dot(
+                pick_ref[part, :], lines[c], preferred_element_type=jnp.float32
+            ).astype(jnp.bfloat16)
+        mine = span(at.me, cap, 16)
+        for k in range(1, plane):
+            j, target = at.in_plane(k)
+            remote(
+                pack.at[slot, span(j, cap, 16)], rows_in.at[c, mine],
+                plane_send.at[c], plane_recv.at[c], target,
+            ).start()
+        rows_in[c, mine, :] = pack[slot, mine, :]
+        logit_ref[...] += jnp.dot(
+            lines[c], router_ref[span(c, cw, cw), :], preferred_element_type=jnp.float32
+        )
+
+    def multiply(c):
+        for copy in weight_copies(c):
+            copy.wait()
+        plane_bulk(c).wait_recv()
+        for b in range(4):
+            part = pl.ds(b * block, block)
+            rows = rows_in[c, part, :]
+            gate_sum[part, :] += jnp.dot(rows, gate[c], preferred_element_type=jnp.float32)
+            up_sum[part, :] += jnp.dot(rows, up[c], preferred_element_type=jnp.float32)
+
+    line_start(0)
+    line_start(1)
+
+    def step(c, carry):
+        @pl.when(c + 2 < chunks)
+        def _():
+            line_start(c + 2)
+
+        line_bulk(c).wait_recv()
+        plane_start(c)
+
+        @pl.when(c >= 1)
+        def _():
+            multiply(c - 1)
+
+        return carry
+
+    lax.fori_loop(0, chunks, step, 0)
+    multiply(chunks - 1)
+    for b in range(4):
+        part = pl.ds(b * block, block)
+        value = gate_sum[part, :]
+        act_ref[part, :] = (value / (1.0 + jnp.exp(-value)) * up_sum[part, :]).astype(jnp.bfloat16)
+
+    def drain(c, carry):
+        line_bulk(c).wait_send()
+        return carry
+
+    lax.fori_loop(0, chunks, drain, 0)
+    plane_bulk(chunks - 2).wait_send()
+    plane_bulk(chunks - 1).wait_send()
+
+
+def return_kernel(
+    line, width, seq_count, cap,
+    act_ref, mix_ref, hidden_ref, down_hbm,
+    out_ref,
+    down, made, rows_in, part_out, own_part, parts_in,
+    plane_send, plane_recv, line_send, line_recv, weight_sem,
+):
+    at = Place(line, width, seq_count)
+    chunks, _, cw = down.shape
+    tokens = hidden_ref.shape[0]
+    plane = at.plane
+    total = plane * cap
+    block = total // 4
+
+    def weight_copy(c):
+        return pltpu.make_async_copy(down_hbm.at[:, span(c, cw, cw)], down.at[c], weight_sem.at[c])
+
+    def start_weights(c, carry):
+        weight_copy(c).start()
+        return carry
+
+    lax.fori_loop(0, chunks, start_weights, 0)
+    at.greet()
+
+    def plane_bulk(c):
+        part = pl.ds(0, (plane - 1) * cap)
+        return remote(
+            made.at[lax.rem(c, 2), part], rows_in.at[c, part],
+            plane_send.at[c], plane_recv.at[c], at.in_plane(1)[1],
+        )
+
+    def line_bulk(c):
+        return remote(
+            part_out.at[lax.rem(c, 2)], parts_in.at[c],
+            line_send.at[c], line_recv.at[c], at.on_line(1)[1],
+        )
+
+    def down_step(c):
+        slot = lax.rem(c, 2)
+        weight_copy(c).wait()
+
+        @pl.when(c >= 2)
+        def _():
+            plane_bulk(c - 2).wait_send()
+
+        for b in range(4):
+            part = pl.ds(b * block, block)
+            made[slot, part, :] = jnp.dot(
+                act_ref[part, :], down[c], preferred_element_type=jnp.float32
+            ).astype(jnp.bfloat16)
+        mine = span(at.me, cap, 16)
+        for k in range(1, plane):
+            j, target = at.in_plane(k)
+            remote(
+                made.at[slot, span(j, cap, 16)], rows_in.at[c, mine],
+                plane_send.at[c], plane_recv.at[c], target,
+            ).start()
+        rows_in[c, mine, :] = made[slot, mine, :]
+
+    def merge_step(c):
+        slot = lax.rem(c, 2)
+        plane_bulk(c).wait_recv()
+
+        @pl.when(c >= 2)
+        def _():
+            line_bulk(c - 2).wait_send()
+
+        for k in range(1, line + 1):
+            z, target = at.on_line(k)
+            part = jnp.dot(
+                mix_ref[span(z, tokens, tokens), :], rows_in[c],
+                preferred_element_type=jnp.float32,
+            )
+            if k == line:
+                own_part[slot] = part
+            else:
+                part_out[slot, k - 1] = part.astype(jnp.bfloat16)
+                remote(
+                    part_out.at[slot, k - 1], parts_in.at[c, k - 1],
+                    line_send.at[c], line_recv.at[c], target,
+                ).start()
+
+    def finish_step(c):
+        line_bulk(c).wait_recv()
+        columns = span(c, cw, cw)
+        value = hidden_ref[:, columns] + own_part[lax.rem(c, 2)]
+        for k in range(line - 1):
+            value += parts_in[c, k].astype(jnp.float32)
+        out_ref[:, columns] = value.astype(jnp.bfloat16)
+
+    def step(c, carry):
+        @pl.when(c < chunks)
+        def _():
+            down_step(c)
+
+        @pl.when((c >= 1) & (c <= chunks))
+        def _():
+            merge_step(c - 1)
+
+        @pl.when(c >= 2)
+        def _():
+            finish_step(c - 2)
+
+        return carry
+
+    lax.fori_loop(0, chunks + 2, step, 0)
+    for c in (chunks - 2, chunks - 1):
+        plane_bulk(c).wait_send()
+        line_bulk(c).wait_send()
+
+
+def kernel_params(collective_id):
+    return pltpu.CompilerParams(
+        collective_id=collective_id, has_side_effects=True, vmem_limit_bytes=VMEM_BYTES
+    )
+
+
+def experts_layer(hidden_state, normed, router_weight, chosen_ids, w_gate, w_up, w_down):
+    seq_count, exp_count = lax.axis_size("seq"), lax.axis_size("exp")
+    tokens, width_d = normed.shape
+    line, width = LINE, exp_count // LINE
+    plane = seq_count * width
+    experts = seq_count * exp_count
+    hidden_units = w_gate.shape[1]
+    per_block = max(2, (tokens * TOP * 9 + 8 * experts - 1) // (8 * experts))
+    cap = (line * per_block + 15) // 16 * 16
+    total = plane * cap
+    group = line * tokens
+    chunks = 8
+    cw = width_d // chunks
+    bf16, f32 = jnp.bfloat16, jnp.float32
+
+    rings = [[z * width + x for z in range(line)] for x in range(width)]
+    ids = lax.all_gather(chosen_ids, "exp", axis_index_groups=rings, tiled=True)
+    named = jnp.any(ids[:, :, None] == jnp.arange(experts, dtype=jnp.int32), axis=1)
+    my_z = lax.axis_index("exp") // width
+    here = lax.dynamic_slice_in_dim(
+        named.reshape(group, seq_count, line, width), my_z, 1, axis=2
+    ).reshape(group, plane)
+    before = jnp.asarray(np.tril(np.ones((group, group)), -1), bf16)
+    rank = jnp.dot(before, here.astype(bf16), preferred_element_type=f32)
+    place = jnp.where(here, rank, -1.0).astype(jnp.int32)
+    seats = jnp.arange(cap, dtype=jnp.int32)
+    pick = (place.T[:, None, :] == seats[None, :, None]).astype(bf16).reshape(total, group)
+
+    vmem = pl.BlockSpec(memory_space=pltpu.VMEM)
+    hbm = pl.BlockSpec(memory_space=pl.ANY)
+    dma = pltpu.SemaphoreType.DMA
+    act, logits = pl.pallas_call(
+        functools.partial(dispatch_kernel, line, width, seq_count, cap),
+        out_shape=(
+            jax.ShapeDtypeStruct((total, hidden_units), bf16),
+            jax.ShapeDtypeStruct((group, experts), f32),
+        ),
+        in_specs=[vmem, vmem, vmem, hbm, hbm],
+        out_specs=(vmem, vmem),
+        scratch_shapes=[
+            pltpu.VMEM((chunks, group, cw), bf16),
+            pltpu.VMEM((2, total, cw), bf16),
+            pltpu.VMEM((chunks, total, cw), bf16),
+            pltpu.VMEM((chunks, cw, hidden_units), bf16),
+            pltpu.VMEM((chunks, cw, hidden_units), bf16),
+            pltpu.VMEM((total, hidden_units), f32),
+            pltpu.VMEM((total, hidden_units), f32),
+            dma((chunks,)), dma((chunks,)), dma((chunks,)), dma((chunks,)), dma((2, chunks)),
+        ],
+        compiler_params=kernel_params(0),
+        name="dispatch",
+    )(normed, pick, router_weight, w_gate, w_up)
+
+    masked = jnp.where(named, logits, -jnp.inf)
+    raised = jnp.exp(masked - jnp.max(masked, axis=1, keepdims=True))
+    route_weight = raised / jnp.sum(raised, axis=1, keepdims=True)
+    weight_here = lax.dynamic_slice_in_dim(
+        route_weight.reshape(group, seq_count, line, width), my_z, 1, axis=2
+    ).reshape(group, plane)
+    mix = jnp.where(place[:, :, None] == seats, weight_here[:, :, None], 0.0)
+    mix = mix.astype(bf16).reshape(group, total)
+
+    return pl.pallas_call(
+        functools.partial(return_kernel, line, width, seq_count, cap),
+        out_shape=jax.ShapeDtypeStruct((tokens, width_d), bf16),
+        in_specs=[vmem, vmem, vmem, hbm],
+        out_specs=vmem,
+        scratch_shapes=[
+            pltpu.VMEM((chunks, hidden_units, cw), bf16),
+            pltpu.VMEM((2, total, cw), bf16),
+            pltpu.VMEM((chunks, total, cw), bf16),
+            pltpu.VMEM((2, line - 1, tokens, cw), bf16),
+            pltpu.VMEM((2, tokens, cw), f32),
+            pltpu.VMEM((chunks, line - 1, tokens, cw), bf16),
+            dma((chunks,)), dma((chunks,)), dma((chunks,)), dma((chunks,)), dma((chunks,)),
+        ],
+        compiler_params=kernel_params(1),
+        name="give_back",
+    )(act, mix, hidden_state, w_down)
 
 
 def per_device(
@@ -90,46 +450,10 @@
     hidden_state = resid[0].astype(jnp.float32) + projected
     mean_square = jnp.mean(hidden_state * hidden_state, axis=1, keepdims=True)
     normed = (hidden_state * lax.rsqrt(mean_square + 1e-06) * norm_gain).astype(jnp.bfloat16)
-    logits = jnp.dot(normed, router_weight, preferred_element_type=jnp.float32)
-    chosen_ids = expert_ids[0]
-    chosen = jnp.take_along_axis(logits, chosen_ids, axis=1)
-    route_weight = jax.nn.softmax(chosen, axis=1)
-    expert_total = seq_count * exp_count
-    capacity = max(2, (token_row_block * TOP * 9 + 8 * expert_total - 1) // (8 * expert_total))
-    flat_ids = chosen_ids.reshape(-1)
-    one_hot = (flat_ids[:, None] == jnp.arange(expert_total, dtype=jnp.int32)[None, :]).astype(
-        jnp.int32
-    )
-    running_rank = jnp.cumsum(one_hot, axis=0) - 1
-    slot_index = jnp.sum(one_hot * running_rank, axis=1)
-    target = flat_ids * capacity + slot_index
-    source_token = jnp.arange(token_row_block * TOP, dtype=jnp.int32) // TOP
-    slot_token = (
-        jnp.full((expert_total * capacity,), token_row_block, jnp.int32)
-        .at[target]
-        .set(source_token)
-    )
-    padded = jnp.concatenate([normed, jnp.zeros((1, model_width), jnp.bfloat16)], axis=0)
-    send_rows = padded[slot_token].reshape(expert_total, capacity, model_width)
-    gate_part = w_gate[0]
-    up_part = w_up[0]
-    down_part = w_down[0]
-    received = lax.all_to_all(send_rows, ("seq", "exp"), split_axis=0, concat_axis=0, tiled=True)
-    flat_rows = received.reshape(-1, model_width)
-    returned = lax.all_to_all(
-        expert_mlp(flat_rows, gate_part, up_part, down_part).reshape(received.shape),
-        ("seq", "exp"),
-        split_axis=0,
-        concat_axis=0,
-        tiled=True,
-    )
-    route_rows = (
-        returned.reshape(-1, model_width)[target]
-        .astype(jnp.float32)
-        .reshape(token_row_block, TOP, model_width)
-    )
-    mixture = jnp.sum(route_weight[:, :, None] * route_rows, axis=1)
-    return (hidden_state + mixture).astype(jnp.bfloat16)[None]
+    out = experts_layer(
+        hidden_state, normed, router_weight, expert_ids[0], w_gate[0], w_up[0], w_down[0]
+    )
+    return out[None]
 
 
 def solution(mesh):

time: 729 us -> 395 us (0.54)
  Pallas kernels: 0 us -> 256 us
  waiting for transfers between devices: 271 us -> 40.3 us
  blocking collectives: 235 us -> 14 us
  local copies, waits for them, and re-layouts: 103 us -> 21.3 us
  matrix products: 54.7 us -> 22.6 us
  other arithmetic: 31.3 us -> 13.9 us
    pallas_call x0 -> x2, Pallas kernels: none -> 256 us  [the longest x1 129 us: experts_layer(): pl.pallas_call(functools.partial(dispatch_kernel, line, width, seq_count,...]
    all_to_all x1 -> x0, blocking collectives: 235 us -> none  [per_device(): lax.all_to_all(send_rows, ('seq', 'exp'), split_axis=0, concat_axis=0, ti...]
    all_to_all x1 -> x0, waiting for transfers between devices: 224 us -> none  [per_device(): lax.all_to_all(expert_mlp(flat_rows, gate_part, up_part, down_part).resha...]
    reshape x4 -> x3, local copies, waits for them, and re-layouts: 52.8 us -> 0.07 us  [the longest x1 0.03 us: experts_layer(): named.reshape(group, seq_count, line, width)]
    gather x6 -> x0, local copies, waits for them, and re-layouts: 35.2 us -> none  [the longest x1 20 us: per_device(): returned.reshape(-1, model_width)[target].astype(jnp.float32)]
    dot_general x4 -> x1, matrix products: 32.3 us -> 0.23 us  [experts_layer(): rank = jnp.dot(before, here.astype(bf16), preferred_element_type=f32)]
    all_gather x0 -> x1, blocking collectives: none -> 14 us  [experts_layer(): ids = lax.all_gather(chosen_ids, 'exp', axis_index_groups=rings, tiled=True)]
    reduce_sum x4 -> x1, other arithmetic: 15.2 us -> 1.19 us  [experts_layer(): route_weight = raised / jnp.sum(raised, axis=1, keepdims=True)]
  transfers between devices with their start and end apart: 5 -> 4, of which waited for: 5 -> 4; matrix products, arithmetic and copies ran while one was open for 4% -> 4% of each run, Pallas kernels for 0% -> 0%
where the time goes in v1:
time: 395 us; the launch traced here: 394 us
  Pallas kernels  256 us (65%)
  waiting for transfers between devices  40.3 us (10%)
  matrix products  22.6 us (6%)
  local copies, waits for them, and re-layouts  21.3 us (5%)
  between operations  14.3 us (4%)
  blocking collectives  14 us (4%)
  other arithmetic  13.9 us (4%)
  starting transfers between devices  11.2 us (3%)
    pallas_call x1, Pallas kernels, experts_layer(): pl.pallas_call(functools.partial(dispatch_kernel, line, width, seq_count,...  129 us
    pallas_call x1, Pallas kernels, experts_layer(): pl.pallas_call(functools.partial(return_kernel, line, width, seq_count, c...  127 us
    reduce_scatter x1, waiting for transfers between devices, per_device(): lax.psum_scatter(jnp.dot(attended, out_weight, preferred_element_type=jnp...  23.1 us
    all_gather x1, blocking collectives, experts_layer(): ids = lax.all_gather(chosen_ids, 'exp', axis_index_groups=rings, tiled=True)  14 us
    all_to_all x1, waiting for transfers between devices, per_device(): lax.all_to_all(query_parts, 'seq', split_axis=1, concat_axis=0, tiled=True)  13.6 us
    dot_general x1, matrix products, per_device(): jnp.dot(attended, out_weight, preferred_element_type=jnp.float32)  9.5 us
  transfers between devices with their start and end apart: 4, of which 4 were waited for; matrix products, arithmetic and copies ran while one was open for 4% of the time, Pallas kernels for 0%

profile of v1, /device:TPU:0, one launch (start us, length us, event | category | flops | bytes accessed | tf_op | source)
XLA Modules:
  0.0 393.6 jit_solution(17179466150905670360)
XLA Ops:
  6.6 0.8 copy-done
  7.9 1.4 gather_fusion
  10.0 4.2 %all-to-all-start = ((bf16[4,64,256]{2,1,0:T(8,128)(2,1)}), bf16[4,64,256]{2,1,0:T(8,128)(2,1)S(1)}, u32[]{:S(2)}, u32[]{:S(2)}) async-start(bf16[4,64,256]{2,1,0:T(8,128)(2,1)} %pad_maximum_fusion.1), calls=%async_computation | async-start | bytes 262144 | tf_op jit(solution)/shard_map/all_to_all | solution.py:418
  14.3 1.0 copy.66
  16.0 1.0 copy.64
  18.9 3.4 all-to-all-start.1
  23.0 0.8 reshape_squeeze.11
  23.8 1.3 copy.68
  25.1 3.3 all-to-all-done.1
  28.3 3.5 all-to-all-start.2
  31.9 0.7 fusion.7
  32.7 13.6 %all-to-all-done.2 = bf16[128,4,1024]{2,0,1:T(8,128)(2,1)S(1)} async-done(((bf16[128,4,1024]{2,0,1:T(8,128)(2,1)}), bf16[128,4,1024]{2,0,1:T(8,128)(2,1)S(1)}, u32[]{:S(2)}, u32[]{:S(2)}) %all-to-all-start.2) | async-done | bytes 1048608 | tf_op jit(solution)/shard_map/all_to_all | solution.py:412
  46.5 7.3 %fusion.33 = (f32[8,512]{1,0:T(8,128)S(1)}, f32[8,512,768]{1,2,0:T(8,128)}) fusion(pred[512,768]{0,1:T(8,128)(4,1)S(1)} %fusion.7, bf16[512,8,128]{2,1,0:T(8,128)(2,1)S(1)} %bitcast.92, bf16[512,128]{1,0:T(8,128)(2,1)S(1)} %get-tuple-element.12, bf16[256,128]{1,0:T(8,128)(2,1)S(1)} %get-tuple-element.14), kind=kOutput, calls=%fused_computation.57 | convolution fusion | flops 818283264 | bytes 14237696 | tf_op jit(solution)/shard_map/sub | solution.py:438
  53.8 5.6 %fusion.8 = bf16[128,8,512]{2,0,1:T(8,128)(2,1)S(1)} fusion(f32[8,512,768]{1,2,0:T(8,128)} %get-tuple-element.16, f32[8,512]{1,0:T(8,128)S(1)} %get-tuple-element.15, bf16[512,128]{1,0:T(8,128)(2,1)S(1)} %get-tuple-element.11, bf16[256,128]{1,0:T(8,128)(2,1)S(1)} %get-tuple-element.13), kind=kOutput, calls=%fused_computation.22 | convolution fusion | flops 812515328 | bytes 13844480 | tf_op jit(solution)/shard_map/htj,jd->thd/dot_general | solution.py:440
  59.4 9.5 %convolution_convert_fusion = bf16[512,4096]{1,0:T(8,128)(2,1)} fusion(bf16[512,1024]{0,1:T(8,128)(2,1)S(1)} %bitcast.102, bf16[1024,4096]{1,0:T(8,128)(2,1)} %param.27), kind=kOutput, calls=%fused_computation.13 | convolution fusion | flops 4297064448 | bytes 13631488 | tf_op jit(solution)/shard_map/dot_general | solution.py:445
  69.6 14.0 %all-gather = s32[1,512,8]{1,2,0:T(8,128)S(1)} all-gather(s32[1,128,8]{1,2,0:T(8,128)S(1)} %copy-done.8), channel_id=2, replica_groups={{0,2,4,6},{1,3,5,7},{8,10,12,14},{9,11,13,15},{16,18,20,22},{17,19,21,2..., dimensions={1}, use_global_device_ids=true | all-gather | bytes 20480 | tf_op jit(solution)/shard_map/all_gather | solution.py:315
  84.1 1.3 copy.72.router_ref
  85.7 1.8 eq.62
  87.4 2.7 copy.73
  90.1 1.3 fusion.6.pick_ref
  91.3 23.1 %reduce-scatter.2.cloned.1.call-done = bf16[128,4096]{1,0:T(8,128)(2,1)} async-done(((bf16[512,4096]{1,0:T(8,128)(2,1)}), bf16[128,4096]{1,0:T(8,128)(2,1)}) %reduce-scatter.2.cloned.1.call-update) | async-done | bytes 1048592 | tf_op jit(solution)/shard_map/reduce_scatter | solution.py:444
  114.4 3.0 convert_add_fusion
  117.4 1.4 multiply_convert_fusion.normed_ref
  118.8 128.6 %dispatch.1 = (bf16[1152,768]{1,0:T(8,128)(2,1)}, f32[512,32]{1,0:T(8,128)}) custom-call(bf16[128,4096]{1,0:T(8,128)(2,1)} %multiply_convert_fusion.normed_ref, bf16[1152,512]{1,0:T(8,128)(2,1)} %fusion.6.pick_ref, bf16[4096,32]{1,0:T(8,128)(2,1)} %copy.72.router_ref, bf16[4096,768]{1,0:T(8,128)(2,1)} %bitcast.87, bf16[4096,768]{1,0:T(8,128)(2,1)} %bitcast.88), custom_call_target="tpu_custom_call" | custom-call | tf_op jit(solution)/shard_map/dispatch/pallas_call | solution.py:330
  247.4 1.1 fusion.24
  248.5 1.2 fusion.21
  249.7 1.2 fusion.20
  251.0 1.1 broadcast_in_dim.95
  252.1 2.4 copy.77
  254.5 2.6 select_convert_fusion.mix_ref
  257.1 127.4 %give_back.1 = bf16[128,4096]{1,0:T(8,128)(2,1)} custom-call(bf16[1152,768]{1,0:T(8,128)(2,1)} %get-tuple-element.7.act_ref, bf16[512,1152]{1,0:T(8,128)(2,1)} %select_convert_fusion.mix_ref, f32[128,4096]{1,0:T(8,128)} %get-tuple-element.9.hidden_ref, bf16[768,4096]{1,0:T(8,128)(2,1)} %bitcast.86), custom_call_target="tpu_custom_call" | custom-call | tf_op jit(solution)/shard_map/give_back/pallas_call | solution.py:361
  384.5 2.3 copy.96
  (47 shorter events, 5.6 us)
Async XLA Ops:
  6.5 0.8 copy-start
  6.5 16.4 %copy-start.4 = (bf16[1,128,4096]{2,1,0:T(8,128)(2,1)S(1)}, bf16[1,128,4096]{2,1,0:T(8,128)(2,1)}, u32[]{:S(2)}) copy-start(bf16[1,128,4096]{2,1,0:T(8,128)(2,1)} %param.21) | copy-start | bytes 3145732
  10.0 8.9 %all-to-all-start = ((bf16[4,64,256]{2,1,0:T(8,128)(2,1)}), bf16[4,64,256]{2,1,0:T(8,128)(2,1)S(1)}, u32[]{:S(2)}, u32[]{:S(2)}) async-start(bf16[4,64,256]{2,1,0:T(8,128)(2,1)} %pad_maximum_fusion.1), calls=%async_computation | async-start | bytes 262144 | tf_op jit(solution)/shard_map/all_to_all | solution.py:418
  18.9 9.4 %all-to-all-start.1 = ((bf16[128,4,256]{2,0,1:T(8,128)(2,1)}), bf16[128,4,256]{2,0,1:T(8,128)(2,1)S(1)}, u32[]{:S(2)}, u32[]{:S(2)}) async-start(bf16[128,4,256]{2,0,1:T(8,128)(2,1)} %pad_maximum_fusion), calls=%async_computation.1 | async-start | bytes 524288 | tf_op jit(solution)/shard_map/all_to_all | solution.py:413
  28.3 18.0 %all-to-all-start.2 = ((bf16[128,4,1024]{2,0,1:T(8,128)(2,1)}), bf16[128,4,1024]{2,0,1:T(8,128)(2,1)S(1)}, u32[]{:S(2)}, u32[]{:S(2)}) async-start(bf16[128,4,1024]{2,0,1:T(8,128)(2,1)} %copy.68), calls=%async_computation.2 | async-start | bytes 2097152 | tf_op jit(solution)/shard_map/all_to_all | solution.py:412
  31.8 82.6 %reduce-scatter.2.cloned.1.call-start = ((), (), s32[]{:S(2)}) async-start(), calls=%async_computation.4 | async-start | bytes 5242880 | tf_op jit(solution)/shard_map/reduce_scatter | solution.py:444
  68.9 0.7 copy-start.8
  68.9 15.2 %copy-start.6 = (bf16[4096,32]{0,1:T(8,128)(2,1)S(1)}, bf16[4096,32]{0,1:T(8,128)(2,1)}, u32[]{:S(2)}) copy-start(bf16[4096,32]{0,1:T(8,128)(2,1)} %param.29) | copy-start | bytes 786436
  68.9 16.5 %copy-start.5 = (bf16[512,512]{1,0:T(8,128)(2,1)S(1)}, bf16[512,512]{1,0:T(8,128)(2,1)}, u32[]{:S(2)}) copy-start(bf16[512,512]{1,0:T(8,128)(2,1)} %constant.50.clone) | copy-start | bytes 1572868
  87.4 27.0 %copy-start.2 = (bf16[1,128,4096]{2,1,0:T(8,128)(2,1)S(1)}, bf16[1,128,4096]{2,1,0:T(8,128)(2,1)}, u32[]{:S(2)}) copy-start(bf16[1,128,4096]{2,1,0:T(8,128)(2,1)} %param.20) | copy-start | bytes 3145732
  91.3 26.1 %copy-start.7 = (f32[4096]{0:T(1024)S(1)}, f32[4096]{0:T(1024)}, u32[]{:S(2)}) copy-start(f32[4096]{0:T(1024)} %param.28) | copy-start | bytes 49156
  114.4 3.0 copy-start.3
  257.1 129.7 %copy-start.1 = (bf16[1,4,64,128]{3,2,1,0:T(8,128)(2,1)S(1)}, bf16[1,4,64,128]{3,2,1,0:T(8,128)(2,1)}, u32[]{:S(2)}) copy-start(bf16[1,4,64,128]{3,2,1,0:T(8,128)(2,1)} %param.25) | copy-start | bytes 196612
Sparse Core Ops, SparseCore 0:
  69.1 45.2 reduce-scatter.1

commit v2 on v1

--- a/solution.py
+++ b/solution.py
@@ -63,10 +63,10 @@
 
 def dispatch_kernel(
     line, width, seq_count, cap,
-    normed_ref, pick_ref, router_ref, gate_hbm, up_hbm,
-    act_ref, logit_ref,
-    lines, pack, rows_in, gate, up, gate_sum, up_sum,
-    line_send, line_recv, plane_send, plane_recv, weight_sem,
+    normed_ref, ids_ref, homes_ref, router_ref, gate_hbm, up_hbm,
+    act_ref, mix_ref,
+    ids, pick, mix_turned, logits, lines, pack, rows_in, gate, up, gate_sum, up_sum,
+    line_send, line_recv, plane_send, plane_recv, weight_sem, ids_send, ids_recv,
 ):
     at = Place(line, width, seq_count)
     chunks, _, cw = lines.shape
@@ -88,12 +88,15 @@
 
     lax.fori_loop(0, chunks, start_weights, 0)
     own = span(at.z, tokens, tokens)
+    ids[own, :] = ids_ref[...]
     for c in range(chunks):
         lines[c, own, :] = normed_ref[:, c * cw : (c + 1) * cw]
     gate_sum[...] = jnp.zeros_like(gate_sum)
     up_sum[...] = jnp.zeros_like(up_sum)
-    logit_ref[...] = jnp.zeros_like(logit_ref)
+    logits[...] = jnp.zeros_like(logits)
     at.greet()
+    for k in range(1, line):
+        remote(ids.at[own], ids.at[own], ids_send, ids_recv, at.on_line(k)[1]).start()
 
     def line_start(c):
         for k in range(1, line):
@@ -122,7 +125,7 @@
         for b in range(4):
             part = pl.ds(b * block, block)
             pack[slot, part, :] = jnp.dot(
-                pick_ref[part, :], lines[c], preferred_element_type=jnp.float32
+                pick[part, :], lines[c], preferred_element_type=jnp.float32
             ).astype(jnp.bfloat16)
         mine = span(at.me, cap, 16)
         for k in range(1, plane):
@@ -132,7 +135,7 @@
                 plane_send.at[c], plane_recv.at[c], target,
             ).start()
         rows_in[c, mine, :] = pack[slot, mine, :]
-        logit_ref[...] += jnp.dot(
+        logits[...] += jnp.dot(
             lines[c], router_ref[span(c, cw, cw), :], preferred_element_type=jnp.float32
         )
 
@@ -146,8 +149,32 @@
             gate_sum[part, :] += jnp.dot(rows, gate[c], preferred_element_type=jnp.float32)
             up_sum[part, :] += jnp.dot(rows, up[c], preferred_element_type=jnp.float32)
 
+    def named(experts):
+        hits = jnp.zeros((ids.shape[0], experts.shape[1]), jnp.float32)
+        for k in range(TOP):
+            hits += jnp.where(ids[:, k : k + 1] == experts, 1.0, 0.0)
+        return hits
+
+    def iota(shape, axis):
+        return lax.broadcasted_iota(jnp.int32, shape, axis)
+
     line_start(0)
     line_start(1)
+    group = ids.shape[0]
+    ids_part = ids.at[pl.ds(0, (line - 1) * tokens)]
+    ids_bulk = remote(ids_part, ids_part, ids_send, ids_recv, at.on_line(1)[1])
+    ids_bulk.wait_recv()
+    experts_here = homes_ref[...] + at.z * width
+    hits = named(experts_here)
+    before = jnp.where(iota((group, group), 1) < iota((group, group), 0), 1.0, 0.0)
+    rank = jnp.dot(
+        before.astype(jnp.bfloat16), hits.astype(jnp.bfloat16), preferred_element_type=jnp.float32
+    )
+    place = jnp.where(hits > 0.0, rank, -1.0).T
+    seats = iota((cap, group), 0).astype(jnp.float32)
+    for j in range(plane):
+        seated = jnp.where(place[j : j + 1, :] == seats, 1.0, 0.0)
+        pick[j * cap : (j + 1) * cap, :] = seated.astype(jnp.bfloat16)
 
     def step(c, carry):
         @pl.when(c + 2 < chunks)
@@ -164,6 +191,21 @@
         return carry
 
     lax.fori_loop(0, chunks, step, 0)
+    experts = logits.shape[1]
+    masked = jnp.where(named(iota((1, experts), 1)) > 0.0, logits[...], -jnp.inf)
+    raised = jnp.exp(masked - jnp.max(masked, axis=1, keepdims=True))
+    weights = raised / jnp.sum(raised, axis=1, keepdims=True)
+    select = jnp.where(iota((experts, experts_here.shape[1]), 0) == experts_here, 1.0, 0.0)
+    weights_here = jnp.dot(
+        weights.astype(jnp.bfloat16), select.astype(jnp.bfloat16),
+        preferred_element_type=jnp.float32,
+    ).T
+    for j in range(plane):
+        seat = pick[j * cap : (j + 1) * cap, :].astype(jnp.float32)
+        mix_turned[j * cap : (j + 1) * cap, :] = weights_here[j : j + 1, :] * seat
+    for b in range(total // 128):
+        part = slice(b * 128, (b + 1) * 128)
+        mix_ref[:, part] = mix_turned[part, :].T.astype(jnp.bfloat16)
     multiply(chunks - 1)
     for b in range(4):
         part = pl.ds(b * block, block)
@@ -175,6 +217,7 @@
         return carry
 
     lax.fori_loop(0, chunks, drain, 0)
+    ids_bulk.wait_send()
     plane_bulk(chunks - 2).wait_send()
     plane_bulk(chunks - 1).wait_send()
 
@@ -307,35 +350,29 @@
     cap = (line * per_block + 15) // 16 * 16
     total = plane * cap
     group = line * tokens
-    chunks = 8
+    chunks = 16
     cw = width_d // chunks
     bf16, f32 = jnp.bfloat16, jnp.float32
 
-    rings = [[z * width + x for z in range(line)] for x in range(width)]
-    ids = lax.all_gather(chosen_ids, "exp", axis_index_groups=rings, tiled=True)
-    named = jnp.any(ids[:, :, None] == jnp.arange(experts, dtype=jnp.int32), axis=1)
-    my_z = lax.axis_index("exp") // width
-    here = lax.dynamic_slice_in_dim(
-        named.reshape(group, seq_count, line, width), my_z, 1, axis=2
-    ).reshape(group, plane)
-    before = jnp.asarray(np.tril(np.ones((group, group)), -1), bf16)
-    rank = jnp.dot(before, here.astype(bf16), preferred_element_type=f32)
-    place = jnp.where(here, rank, -1.0).astype(jnp.int32)
-    seats = jnp.arange(cap, dtype=jnp.int32)
-    pick = (place.T[:, None, :] == seats[None, :, None]).astype(bf16).reshape(total, group)
+    homes = np.full((1, 128), -experts, np.int32)
+    homes[0, :plane] = [j // width * exp_count + j % width for j in range(plane)]
 
     vmem = pl.BlockSpec(memory_space=pltpu.VMEM)
     hbm = pl.BlockSpec(memory_space=pl.ANY)
     dma = pltpu.SemaphoreType.DMA
-    act, logits = pl.pallas_call(
+    act, mix = pl.pallas_call(
         functools.partial(dispatch_kernel, line, width, seq_count, cap),
         out_shape=(
             jax.ShapeDtypeStruct((total, hidden_units), bf16),
-            jax.ShapeDtypeStruct((group, experts), f32),
+            jax.ShapeDtypeStruct((group, total), bf16),
         ),
-        in_specs=[vmem, vmem, vmem, hbm, hbm],
+        in_specs=[vmem, vmem, vmem, vmem, hbm, hbm],
         out_specs=(vmem, vmem),
         scratch_shapes=[
+            pltpu.VMEM((group, TOP), jnp.int32),
+            pltpu.VMEM((total, group), bf16),
+            pltpu.VMEM((total, group), f32),
+            pltpu.VMEM((group, experts), f32),
             pltpu.VMEM((chunks, group, cw), bf16),
             pltpu.VMEM((2, total, cw), bf16),
             pltpu.VMEM((chunks, total, cw), bf16),
@@ -344,19 +381,11 @@
             pltpu.VMEM((total, hidden_units), f32),
             pltpu.VMEM((total, hidden_units), f32),
             dma((chunks,)), dma((chunks,)), dma((chunks,)), dma((chunks,)), dma((2, chunks)),
+            dma, dma,
         ],
         compiler_params=kernel_params(0),
         name="dispatch",
-    )(normed, pick, router_weight, w_gate, w_up)
-
-    masked = jnp.where(named, logits, -jnp.inf)
-    raised = jnp.exp(masked - jnp.max(masked, axis=1, keepdims=True))
-    route_weight = raised / jnp.sum(raised, axis=1, keepdims=True)
-    weight_here = lax.dynamic_slice_in_dim(
-        route_weight.reshape(group, seq_count, line, width), my_z, 1, axis=2
-    ).reshape(group, plane)
-    mix = jnp.where(place[:, :, None] == seats, weight_here[:, :, None], 0.0)
-    mix = mix.astype(bf16).reshape(group, total)
+    )(normed, chosen_ids, jnp.asarray(homes), router_weight, w_gate, w_up)
 
     return pl.pallas_call(
         functools.partial(return_kernel, line, width, seq_count, cap),

time: 395 us -> 379 us (0.959)
  waiting for transfers between devices: 40.3 us -> 59.5 us
  blocking collectives: 14 us -> 0 us
  local copies, waits for them, and re-layouts: 21.3 us -> 14.1 us
  Pallas kernels: 256 us -> 249 us
  other arithmetic: 13.9 us -> 7.68 us
    reduce_scatter x1, waiting for transfers between devices: 23.1 us -> 43.4 us  [per_device(): lax.psum_scatter(jnp.dot(attended, out_weight, preferred_element_type=jnp...]
    all_gather x1 -> x0, blocking collectives: 14 us -> none  [experts_layer(): ids = lax.all_gather(chosen_ids, 'exp', axis_index_groups=rings, tiled=True)]
    pallas_call x1, Pallas kernels: 127 us -> 122 us  [experts_layer(): pl.pallas_call(functools.partial(return_kernel, line, width, seq_count, c...]
    eq x4 -> x0, local copies, waits for them, and re-layouts: 4.5 us -> none  [the longest x2 4.42 us: experts_layer(): mix = jnp.where(place[:, :, None] == seats, weight_here[:, :, None], 0.0)]
  transfers between devices with their start and end apart: 4 -> 4, of which waited for: 4 -> 4; matrix products, arithmetic and copies ran while one was open for 4% -> 3% of each run, Pallas kernels for 0% -> 0%
where the time goes in v2:
time: 379 us; the launch traced here: 378 us
  Pallas kernels  249 us (66%)
  waiting for transfers between devices  59.5 us (16%)
  matrix products  22.4 us (6%)
  between operations  14.2 us (4%)
  local copies, waits for them, and re-layouts  14.1 us (4%)
  starting transfers between devices  11.2 us (3%)
  other arithmetic  7.68 us (2%)
    pallas_call x1, Pallas kernels, experts_layer(): pl.pallas_call(functools.partial(dispatch_kernel, line, width, seq_count,...  127 us
    pallas_call x1, Pallas kernels, experts_layer(): pl.pallas_call(functools.partial(return_kernel, line, width, seq_count, c...  122 us
    reduce_scatter x1, waiting for transfers between devices, per_device(): lax.psum_scatter(jnp.dot(attended, out_weight, preferred_element_type=jnp...  43.4 us
    all_to_all x1, waiting for transfers between devices, per_device(): lax.all_to_all(query_parts, 'seq', split_axis=1, concat_axis=0, tiled=True)  13.6 us
    dot_general x1, matrix products, per_device(): jnp.dot(attended, out_weight, preferred_element_type=jnp.float32)  9.53 us
  transfers between devices with their start and end apart: 4, of which 4 were waited for; matrix products, arithmetic and copies ran while one was open for 3% of the time, Pallas kernels for 0%

profile of v2, /device:TPU:0, one launch (start us, length us, event | category | flops | bytes accessed | tf_op | source)
XLA Modules:
  0.0 377.9 jit_solution(8758244561467936518)
XLA Ops:
  6.5 0.8 copy-done
  7.4 0.6 gather_fusion
  7.9 1.4 gather_fusion.1
  9.3 0.7 pad_maximum_fusion.1
  10.0 4.2 %all-to-all-start = ((bf16[4,64,256]{2,1,0:T(8,128)(2,1)}), bf16[4,64,256]{2,1,0:T(8,128)(2,1)S(1)}, u32[]{:S(2)}, u32[]{:S(2)}) async-start(bf16[4,64,256]{2,1,0:T(8,128)(2,1)} %pad_maximum_fusion.1), calls=%async_computation | async-start | bytes 262144 | tf_op jit(solution)/shard_map/all_to_all | solution.py:447
  14.3 1.0 copy.31
  15.3 0.1 copy.32
  15.4 0.6 gather_fusion.2
  16.0 1.0 copy.33
  17.0 0.1 copy.34
  17.2 0.6 gather_fusion.3
  17.8 0.7 pad_maximum_fusion
  18.5 0.4 all-to-all-done
  18.9 3.4 all-to-all-start.1
  23.0 1.9 reshape_squeeze.11
  24.8 1.3 copy.35
  26.1 2.2 all-to-all-done.1
  28.3 3.5 all-to-all-start.2
  31.9 0.7 fusion.6
  32.7 13.6 %all-to-all-done.2 = bf16[128,4,1024]{2,0,1:T(8,128)(2,1)S(1)} async-done(((bf16[128,4,1024]{2,0,1:T(8,128)(2,1)}), bf16[128,4,1024]{2,0,1:T(8,128)(2,1)S(1)}, u32[]{:S(2)}, u32[]{:S(2)}) %all-to-all-start.2) | async-done | bytes 1048608 | tf_op jit(solution)/shard_map/all_to_all | solution.py:441
  46.3 0.3 copy.44
  46.5 7.3 %fusion.27 = (f32[8,512]{1,0:T(8,128)S(1)}, f32[8,512,768]{1,2,0:T(8,128)}) fusion(pred[512,768]{0,1:T(8,128)(4,1)S(1)} %fusion.6, bf16[512,8,128]{2,1,0:T(8,128)(2,1)S(1)} %bitcast.73, bf16[512,128]{1,0:T(8,128)(2,1)S(1)} %get-tuple-element.12, bf16[256,128]{1,0:T(8,128)(2,1)S(1)} %get-tuple-element.14), kind=kOutput, calls=%fused_computation.43 | convolution fusion | flops 818283264 | bytes 14237696 | tf_op jit(solution)/shard_map/sub | solution.py:467
  53.8 5.6 %fusion.7 = bf16[128,8,512]{2,0,1:T(8,128)(2,1)S(1)} fusion(f32[8,512,768]{1,2,0:T(8,128)} %get-tuple-element.16, f32[8,512]{1,0:T(8,128)S(1)} %get-tuple-element.15, bf16[512,128]{1,0:T(8,128)(2,1)S(1)} %get-tuple-element.11, bf16[256,128]{1,0:T(8,128)(2,1)S(1)} %get-tuple-element.13), kind=kOutput, calls=%fused_computation.19 | convolution fusion | flops 812515328 | bytes 13844480 | tf_op jit(solution)/shard_map/htj,jd->thd/dot_general | solution.py:469
  59.4 9.5 %convolution_convert_fusion = bf16[512,4096]{1,0:T(8,128)(2,1)} fusion(bf16[512,1024]{0,1:T(8,128)(2,1)S(1)} %bitcast.82, bf16[1024,4096]{1,0:T(8,128)(2,1)} %param.27), kind=kOutput, calls=%fused_computation.13 | convolution fusion | flops 4297064448 | bytes 13631488 | tf_op jit(solution)/shard_map/dot_general | solution.py:474
  69.0 1.4 copy.40.router_ref
  70.4 0.7 copy.39
  71.1 43.4 %reduce-scatter.2.cloned.1.call-done = bf16[128,4096]{1,0:T(8,128)(2,1)} async-done(((bf16[512,4096]{1,0:T(8,128)(2,1)}), bf16[128,4096]{1,0:T(8,128)(2,1)}) %reduce-scatter.2.cloned.1.call-update) | async-done | bytes 1048592 | tf_op jit(solution)/shard_map/reduce_scatter | solution.py:473
  114.5 2.9 convert_add_fusion
  117.4 2.6 multiply_convert_fusion.normed_ref
  120.0 126.5 %dispatch.1 = (bf16[1152,768]{1,0:T(8,128)(2,1)}, bf16[512,1152]{1,0:T(8,128)(2,1)}) custom-call(bf16[128,4096]{1,0:T(8,128)(2,1)} %multiply_convert_fusion.normed_ref, s32[128,8]{1,0:T(8,128)} %bitcast.80, s32[1,128]{1,0:T(1,128)} %constant.26.clone.homes_ref, bf16[4096,32]{1,0:T(8,128)(2,1)} %copy.40.router_ref, bf16[4096,768]{1,0:T(8,128)(2,1)} %bitcast.68, ...), custom_call_target="tpu_custom_call" | custom-call | tf_op jit(solution)/shard_map/dispatch/pallas_call | solution.py:363
  246.5 122.2 %give_back.1 = bf16[128,4096]{1,0:T(8,128)(2,1)} custom-call(bf16[1152,768]{1,0:T(8,128)(2,1)} %get-tuple-element.7.act_ref, bf16[512,1152]{1,0:T(8,128)(2,1)} %get-tuple-element.8.mix_ref, f32[128,4096]{1,0:T(8,128)} %get-tuple-element.9.hidden_ref, bf16[768,4096]{1,0:T(8,128)(2,1)} %bitcast.70), custom_call_target="tpu_custom_call" | custom-call | tf_op jit(solution)/shard_map/give_back/pallas_call | solution.py:390
  368.7 2.3 copy.59
  (18 shorter events, 0.1 us)
Async XLA Ops:
  6.5 0.8 copy-start
  10.0 8.9 %all-to-all-start = ((bf16[4,64,256]{2,1,0:T(8,128)(2,1)}), bf16[4,64,256]{2,1,0:T(8,128)(2,1)S(1)}, u32[]{:S(2)}, u32[]{:S(2)}) async-start(bf16[4,64,256]{2,1,0:T(8,128)(2,1)} %pad_maximum_fusion.1), calls=%async_computation | async-start | bytes 262144 | tf_op jit(solution)/shard_map/all_to_all | solution.py:447
  18.9 9.4 %all-to-all-start.1 = ((bf16[128,4,256]{2,0,1:T(8,128)(2,1)}), bf16[128,4,256]{2,0,1:T(8,128)(2,1)S(1)}, u32[]{:S(2)}, u32[]{:S(2)}) async-start(bf16[128,4,256]{2,0,1:T(8,128)(2,1)} %pad_maximum_fusion), calls=%async_computation.1 | async-start | bytes 524288 | tf_op jit(solution)/shard_map/all_to_all | solution.py:442
  28.3 18.0 %all-to-all-start.2 = ((bf16[128,4,1024]{2,0,1:T(8,128)(2,1)}), bf16[128,4,1024]{2,0,1:T(8,128)(2,1)S(1)}, u32[]{:S(2)}, u32[]{:S(2)}) async-start(bf16[128,4,1024]{2,0,1:T(8,128)(2,1)} %copy.35), calls=%async_computation.2 | async-start | bytes 2097152 | tf_op jit(solution)/shard_map/all_to_all | solution.py:441
  31.8 82.6 %reduce-scatter.2.cloned.1.call-start = ((), (), s32[]{:S(2)}) async-start(), calls=%async_computation.4 | async-start | bytes 5242880 | tf_op jit(solution)/shard_map/reduce_scatter | solution.py:473
  59.4 9.6 %copy-start.2 = (bf16[4096,32]{0,1:T(8,128)(2,1)S(1)}, bf16[4096,32]{0,1:T(8,128)(2,1)}, u32[]{:S(2)}) copy-start(bf16[4096,32]{0,1:T(8,128)(2,1)} %param.29) | copy-start | bytes 786436
  59.4 10.9 %copy-start.4 = (s32[1,128,8]{1,2,0:T(8,128)S(1)}, s32[1,128,8]{1,2,0:T(8,128)}, u32[]{:S(2)}) copy-start(s32[1,128,8]{1,2,0:T(8,128)} %param.30) | copy-start | bytes 12292
  69.0 45.5 %copy-start.1 = (bf16[1,128,4096]{2,1,0:T(8,128)(2,1)S(1)}, bf16[1,128,4096]{2,1,0:T(8,128)(2,1)}, u32[]{:S(2)}) copy-start(bf16[1,128,4096]{2,1,0:T(8,128)(2,1)} %param.20) | copy-start | bytes 3145732
  69.0 48.4 %copy-start.3 = (f32[4096]{0:T(1024)S(1)}, f32[4096]{0:T(1024)}, u32[]{:S(2)}) copy-start(f32[4096]{0:T(1024)} %param.28) | copy-start | bytes 49156
Sparse Core Ops, SparseCore 0:
  69.1 45.3 reduce-scatter.1

commit v3 on v2

--- a/solution.py
+++ b/solution.py
@@ -406,6 +406,191 @@
     )(act, mix, hidden_state, w_down)
 
 
+def attend_kernel(
+    heads, group_length, prefix_total,
+    queries_ref, keys_ref, values_ref, key_cache_ref, value_cache_ref, bias_ref, resid_ref,
+    gain_ref, out_hbm,
+    hidden_ref, normed_ref,
+    query, key, value, mask, attended, weight, pair_out, pair_in, own_sum, far_out, far_in,
+    key_send, key_recv, value_send, value_recv, query_send, query_recv,
+    pair_send, pair_recv, far_send, far_recv, weight_sem,
+):
+    seq_count = lax.axis_size("seq")
+    me = lax.axis_index("seq")
+    core, chip = lax.rem(me, 2), lax.div(me, 2)
+    partner = {"seq": 2 * chip + 1 - core}
+    chips = seq_count // 2
+    tokens = queries_ref.shape[0]
+    cached = key_cache_ref.shape[1]
+    chunks, _, cw = weight.shape
+    bf16, f32 = jnp.bfloat16, jnp.float32
+
+    def weight_copy(c):
+        return pltpu.make_async_copy(out_hbm.at[:, span(c, cw, cw)], weight.at[c], weight_sem.at[c])
+
+    def start_weights(c, carry):
+        weight_copy(c).start()
+        return carry
+
+    lax.fori_loop(0, chunks, start_weights, 0)
+    barrier = pltpu.get_barrier_semaphore()
+    for k in range(1, seq_count):
+        pl.semaphore_signal(
+            barrier, inc=1, device_id={"seq": lax.rem(me + k, seq_count)}, device_id_type=MESH
+        )
+    pl.semaphore_wait(barrier, seq_count - 1)
+
+    def head_of(peer):
+        return lax.div(peer * heads, group_length)
+
+    span_rows = pl.ds(pl.multiple_of(prefix_total + me * tokens, 16), tokens)
+    cache_rows = span(me, cached, 16)
+    own_rows = span(me, tokens, tokens)
+    for k in range(1, seq_count):
+        peer = lax.rem(me + k, seq_count)
+        target = {"seq": peer}
+        columns = span(head_of(peer), HEAD_SIZE, HEAD_SIZE)
+        for new, cache, full, send, recv in (
+            (keys_ref, key_cache_ref, key, key_send, key_recv),
+            (values_ref, value_cache_ref, value, value_send, value_recv),
+        ):
+            remote(new.at[:, columns], full.at[span_rows], send, recv, target).start()
+            remote(cache.at[head_of(peer)], full.at[cache_rows], send, recv, target).start()
+
+    def start_queries(h, carry):
+        for k in range(1, seq_count):
+            peer = lax.rem(me + k, seq_count)
+            remote(
+                queries_ref.at[:, span(peer * heads + h, HEAD_SIZE, HEAD_SIZE)],
+                query.at[h, own_rows], query_send.at[h], query_recv.at[h], {"seq": peer},
+            ).start()
+        query[h, own_rows, :] = queries_ref[:, span(me * heads + h, HEAD_SIZE, HEAD_SIZE)]
+        return carry
+
+    lax.fori_loop(0, heads, start_queries, 0)
+    my_columns = span(head_of(me), HEAD_SIZE, HEAD_SIZE)
+    key[span_rows, :] = keys_ref[:, my_columns]
+    value[span_rows, :] = values_ref[:, my_columns]
+    key[cache_rows, :] = key_cache_ref[head_of(me)]
+    value[cache_rows, :] = value_cache_ref[head_of(me)]
+    length = mask.shape[0]
+    mask[:, :prefix_total] = jnp.broadcast_to(bias_ref[...], (length, prefix_total))
+    later = lax.broadcasted_iota(jnp.int32, (length, length), 1) > lax.broadcasted_iota(
+        jnp.int32, (length, length), 0
+    )
+    mask[:, prefix_total:] = jnp.where(later, -1e30, 0.0)
+
+    def bulk(full, send, recv):
+        part = full.at[pl.ds(0, (seq_count - 1) * (tokens + cached))]
+        return remote(part, part, send, recv, {"seq": lax.rem(me + 1, seq_count)})
+
+    key_bulk = bulk(key, key_send, key_recv)
+    value_bulk = bulk(value, value_send, value_recv)
+    key_bulk.wait_recv()
+    value_bulk.wait_recv()
+
+    def query_bulk(h):
+        part = query.at[h, pl.ds(0, (seq_count - 1) * tokens)]
+        return remote(
+            part, part, query_send.at[h], query_recv.at[h], {"seq": lax.rem(me + 1, seq_count)}
+        )
+
+    def attend_head(h, carry):
+        query_bulk(h).wait_recv()
+        for b in range(seq_count):
+            rows = slice(b * tokens, (b + 1) * tokens)
+            reach = prefix_total + (b + 1) * tokens
+            scores = lax.dot_general(
+                query[h, rows, :], key[:reach, :], (((1,), (1,)), ((), ())),
+                preferred_element_type=f32,
+            ) * HEAD_SIZE ** (-0.5) + mask[rows, :reach]
+            raised = jnp.exp(scores - jnp.max(scores, axis=1, keepdims=True))
+            mixed = jnp.dot(raised.astype(bf16), value[:reach, :], preferred_element_type=f32)
+            mixed = mixed / jnp.sum(raised, axis=1, keepdims=True)
+            attended[rows, span(h, HEAD_SIZE, HEAD_SIZE)] = mixed.astype(bf16)
+        return carry
+
+    lax.fori_loop(0, heads, attend_head, 0)
+
+    def pair_bulk(c):
+        return remote(pair_out.at[c], pair_in.at[c], pair_send.at[c], pair_recv.at[c], partner)
+
+    def far_bulk(c):
+        return remote(far_out.at[c], far_in.at[c], far_send.at[c], far_recv.at[c], partner)
+
+    def project(c, owner):
+        rows = span(owner, tokens, tokens)
+        return jnp.dot(attended[rows, :], weight[c], preferred_element_type=f32)
+
+    def pair_step(c):
+        weight_copy(c).wait()
+        for k in range(chips):
+            there = lax.rem(chip + k, chips)
+            pair_out[c, k] = project(c, 2 * there + 1 - core).astype(bf16)
+        pair_bulk(c).start()
+        for k in range(chips):
+            there = lax.rem(chip + k, chips)
+            own_sum[lax.rem(c, 2), k] = project(c, 2 * there + core)
+
+    def far_step(c):
+        pair_bulk(c).wait_recv()
+        for k in range(1, chips):
+            there = lax.rem(chip + k, chips)
+            both = own_sum[lax.rem(c, 2), k] + pair_in[c, k].astype(f32)
+            far_out[c, k - 1] = both.astype(bf16)
+            remote(
+                far_out.at[c, k - 1], far_in.at[c, k - 1], far_send.at[c], far_recv.at[c],
+                {"seq": 2 * there + core},
+            ).start()
+        columns = span(c, cw, cw)
+        hidden_ref[:, columns] = (
+            resid_ref[:, columns].astype(f32) + own_sum[lax.rem(c, 2), 0] + pair_in[c, 0].astype(f32)
+        )
+
+    def step(c, carry):
+        @pl.when(c < chunks)
+        def _():
+            pair_step(c)
+
+        @pl.when(c >= 1)
+        def _():
+            far_step(c - 1)
+
+        return carry
+
+    lax.fori_loop(0, chunks + 1, step, 0)
+
+    def sum_step(c, square):
+        far_bulk(c).wait_recv()
+        columns = span(c, cw, cw)
+        total = hidden_ref[:, columns]
+        for k in range(chips - 1):
+            total += far_in[c, k].astype(f32)
+        hidden_ref[:, columns] = total
+        return square + jnp.sum(total * total, axis=1, keepdims=True)
+
+    square = lax.fori_loop(0, chunks, sum_step, jnp.zeros((tokens, 1), f32))
+    factor = lax.rsqrt(square / hidden_ref.shape[1] + 1e-06)
+    for c in range(chunks):
+        columns = slice(c * cw, (c + 1) * cw)
+        normed_ref[:, columns] = (hidden_ref[:, columns] * factor * gain_ref[:, columns]).astype(bf16)
+
+    key_bulk.wait_send()
+    value_bulk.wait_send()
+
+    def drain_queries(h, carry):
+        query_bulk(h).wait_send()
+        return carry
+
+    def drain(c, carry):
+        pair_bulk(c).wait_send()
+        far_bulk(c).wait_send()
+        return carry
+
+    lax.fori_loop(0, heads, drain_queries, 0)
+    lax.fori_loop(0, chunks, drain, 0)
+
+
 def per_device(
     resid,
     queries,
@@ -423,62 +608,50 @@
     w_down,
 ):
     seq_count = lax.axis_size("seq")
-    exp_count = lax.axis_size("exp")
-    token_row_block = queries.shape[1]
-    model_width = resid.shape[2]
-    heads_here = QUERY_HEAD_HALF // seq_count
+    tokens, model_width = resid.shape[1:]
+    heads = QUERY_HEAD_HALF // seq_count
     group_length = QUERY_HEAD_HALF // KEY_VALUE_HEADS
-    key_value_choice = np.arange(seq_count) * heads_here // group_length
-    query_parts = queries[0].reshape(token_row_block, seq_count, heads_here * HEAD_SIZE)
-    newest_keys = span_rotated_keys[0].reshape(token_row_block, KEY_VALUE_HEADS, HEAD_SIZE)[
-        :, key_value_choice, :
-    ]
-    newest_values = span_value_rows[0].reshape(token_row_block, KEY_VALUE_HEADS, HEAD_SIZE)[
-        :, key_value_choice, :
-    ]
-    fresh_pairs = jnp.concatenate([newest_keys, newest_values], axis=2)
-    query_heads, span_pairs = (
-        lax.all_to_all(query_parts, "seq", split_axis=1, concat_axis=0, tiled=True),
-        lax.all_to_all(fresh_pairs, "seq", split_axis=1, concat_axis=0, tiled=True),
-    )
-    cache_pairs = jnp.concatenate(
-        [key_cache[0][key_value_choice], prefix_value_cache[0][key_value_choice]], axis=2
-    )
-    prefix_pairs = lax.all_to_all(cache_pairs, "seq", split_axis=0, concat_axis=1, tiled=True)[0]
-    span_length = query_heads.shape[0]
-    prefix_total = prefix_pairs.shape[0]
-    all_keys = jnp.concatenate([prefix_pairs[:, :HEAD_SIZE], span_pairs[:, 0, :HEAD_SIZE]], axis=0)
-    all_values = jnp.concatenate(
-        [prefix_pairs[:, HEAD_SIZE:], span_pairs[:, 0, HEAD_SIZE:]], axis=0
-    )
-    query_block = query_heads.reshape(span_length, heads_here, HEAD_SIZE)
-    scores = jnp.einsum(
-        "thd,jd->htj", query_block, all_keys, preferred_element_type=jnp.float32
-    ) * HEAD_SIZE ** (-0.5)
-    position = jnp.arange(prefix_total + span_length, dtype=jnp.int32)
-    query_pos = jnp.arange(span_length, dtype=jnp.int32)
-    usable_keys = jnp.where(
-        position[None, :] < prefix_total,
-        position[None, :] < prefix_len[0],
-        position[None, :] - prefix_total <= query_pos[:, None],
-    )
-    scores = jnp.where(usable_keys[None], scores, -1e30)
-    top_score = jnp.max(scores, axis=2, keepdims=True)
-    raised = jnp.exp(scores - top_score)
-    attn_weights = (raised / jnp.sum(raised, axis=2, keepdims=True)).astype(jnp.bfloat16)
-    attended = jnp.einsum(
-        "htj,jd->thd", attn_weights, all_values, preferred_element_type=jnp.float32
-    ).astype(jnp.bfloat16)
-    attended = attended.reshape(span_length, heads_here * HEAD_SIZE)
-    projected = lax.psum_scatter(
-        jnp.dot(attended, out_weight, preferred_element_type=jnp.float32).astype(jnp.bfloat16),
-        "seq",
-        scatter_dimension=0,
-        tiled=True,
-    ).astype(jnp.float32)
-    hidden_state = resid[0].astype(jnp.float32) + projected
-    mean_square = jnp.mean(hidden_state * hidden_state, axis=1, keepdims=True)
-    normed = (hidden_state * lax.rsqrt(mean_square + 1e-06) * norm_gain).astype(jnp.bfloat16)
+    prefix_total = key_cache.shape[2] * seq_count
+    length = tokens * seq_count
+    chips = seq_count // 2
+    chunks = 8
+    cw = model_width // chunks
+    bf16, f32 = jnp.bfloat16, jnp.float32
+    live = jnp.arange(prefix_total, dtype=jnp.int32) < prefix_len[0]
+    bias = jnp.where(live, 0.0, -1e30).astype(f32)[None]
+
+    vmem = pl.BlockSpec(memory_space=pltpu.VMEM)
+    hbm = pl.BlockSpec(memory_space=pl.ANY)
+    dma = pltpu.SemaphoreType.DMA
+    hidden_state, normed = pl.pallas_call(
+        functools.partial(attend_kernel, heads, group_length, prefix_total),
+        out_shape=(
+            jax.ShapeDtypeStruct((tokens, model_width), f32),
+            jax.ShapeDtypeStruct((tokens, model_width), bf16),
+        ),
+        in_specs=[vmem] * 8 + [hbm],
+        out_specs=(vmem, vmem),
+        scratch_shapes=[
+            pltpu.VMEM((heads, length, HEAD_SIZE), bf16),
+            pltpu.VMEM((prefix_total + length, HEAD_SIZE), bf16),
+            pltpu.VMEM((prefix_total + length, HEAD_SIZE), bf16),
+            pltpu.VMEM((length, prefix_total + length), f32),
+            pltpu.VMEM((length, heads * HEAD_SIZE), bf16),
+            pltpu.VMEM((chunks, heads * HEAD_SIZE, cw), bf16),
+            pltpu.VMEM((chunks, chips, tokens, cw), bf16),
+            pltpu.VMEM((chunks, chips, tokens, cw), bf16),
+            pltpu.VMEM((2, chips, tokens, cw), f32),
+            pltpu.VMEM((chunks, chips - 1, tokens, cw), bf16),
+            pltpu.VMEM((chunks, chips - 1, tokens, cw), bf16),
+            dma, dma, dma, dma, dma((heads,)), dma((heads,)),
+            dma((chunks,)), dma((chunks,)), dma((chunks,)), dma((chunks,)), dma((chunks,)),
+        ],
+        compiler_params=kernel_params(2),
+        name="attend",
+    )(
+        queries[0], span_rotated_keys[0], span_value_rows[0], key_cache[0],
+        prefix_value_cache[0], bias, resid[0], norm_gain[None], out_weight,
+    )
     out = experts_layer(
         hidden_state, normed, router_weight, expert_ids[0], w_gate[0], w_up[0], w_down[0]
     )

time: 379 us -> 309 us (0.82)
  waiting for transfers between devices: 59.5 us -> 0 us
  Pallas kernels: 249 us -> 301 us
  matrix products: 22.4 us -> 0 us
  between operations: 14.2 us -> 0.68 us
  starting transfers between devices: 11.2 us -> 0 us
  local copies, waits for them, and re-layouts: 14.1 us -> 5.95 us
  other arithmetic: 7.68 us -> 0.6 us
    pallas_call x0 -> x1, Pallas kernels: none -> 52.5 us  [per_device(): pl.pallas_call(functools.partial(attend_kernel, heads, group_length, pref...]
    reduce_scatter x1 -> x0, waiting for transfers between devices: 43.4 us -> none  [per_device(): lax.psum_scatter(jnp.dot(attended, out_weight, preferred_element_type=jnp...]
    all_to_all x3 -> x0, waiting for transfers between devices: 16.2 us -> none  [the longest x1 13.6 us: per_device(): lax.all_to_all(query_parts, 'seq', split_axis=1, concat_axis=0, tiled=True)]
    dot_general x2 -> x0, matrix products: 15.1 us -> none  [the longest x1 9.53 us: per_device(): jnp.dot(attended, out_weight, preferred_element_type=jnp.float32)]
    all_to_all x3 -> x0, starting transfers between devices: 11.2 us -> none  [the longest x1 4.24 us: per_device(): lax.all_to_all(cache_pairs, 'seq', split_axis=0, concat_axis=1, tiled=True)]
    sub x1 -> x0, matrix products: 7.27 us -> none  [per_device(): raised = jnp.exp(scores - top_score)]
  transfers between devices with their start and end apart: 4 -> 0, of which waited for: 4 -> 0; matrix products, arithmetic and copies ran while one was open for 3% -> 0% of each run, Pallas kernels for 0% -> 0%
where the time goes in v3:
time: 309 us
  Pallas kernels  301 us (97%)
  local copies, waits for them, and re-layouts  5.95 us (2%)
    pallas_call x1, Pallas kernels, experts_layer(): pl.pallas_call(functools.partial(dispatch_kernel, line, width, seq_count,...  127 us
    pallas_call x1, Pallas kernels, experts_layer(): pl.pallas_call(functools.partial(return_kernel, line, width, seq_count, c...  122 us
    pallas_call x1, Pallas kernels, per_device(): pl.pallas_call(functools.partial(attend_kernel, heads, group_length, pref...  52.5 us

profile of v3, /device:TPU:0, one launch (start us, length us, event | category | flops | bytes accessed | tf_op | source)
XLA Modules:
  0.0 308.6 jit_solution(3796233139070736686)
XLA Ops:
  0.7 0.6 compare_select_fusion.bias_ref
  1.3 1.4 copy.16
  2.7 2.3 copy.17.router_ref
  4.9 52.5 %attend.1 = (f32[128,4096]{1,0:T(8,128)}, bf16[128,4096]{1,0:T(8,128)(2,1)}) custom-call(bf16[128,4096]{1,0:T(8,128)(2,1)} %bitcast.18, bf16[128,512]{1,0:T(8,128)(2,1)} %bitcast.21, bf16[128,512]{1,0:T(8,128)(2,1)} %bitcast.22, bf16[4,64,128]{2,1,0:T(8,128)(2,1)} %bitcast.23, bf16[4,64,128]{2,1,0:T(8,128)(2,1)} %bitcast.24, ...), custom_call_target="tpu_custom_call" | custom-call | tf_op jit(solution)/shard_map/attend/pallas_call | solution.py:626
  57.4 126.9 %dispatch.1 = (bf16[1152,768]{1,0:T(8,128)(2,1)}, bf16[512,1152]{1,0:T(8,128)(2,1)}) custom-call(bf16[128,4096]{1,0:T(8,128)(2,1)} %get-tuple-element.9.normed_ref, s32[128,8]{1,0:T(8,128)} %bitcast.20, s32[1,128]{1,0:T(1,128)} %constant.6.clone.homes_ref, bf16[4096,32]{1,0:T(8,128)(2,1)} %copy.17.router_ref, bf16[4096,768]{1,0:T(8,128)(2,1)} %bitcast.14, ...), custom_call_target="tpu_custom_call" | custom-call | tf_op jit(solution)/shard_map/dispatch/pallas_call | solution.py:363
  184.3 122.0 %give_back.1 = bf16[128,4096]{1,0:T(8,128)(2,1)} custom-call(bf16[1152,768]{1,0:T(8,128)(2,1)} %get-tuple-element.10.act_ref, bf16[512,1152]{1,0:T(8,128)(2,1)} %get-tuple-element.11.mix_ref, f32[128,4096]{1,0:T(8,128)} %get-tuple-element.12.hidden_ref, bf16[768,4096]{1,0:T(8,128)(2,1)} %bitcast.16), custom_call_target="tpu_custom_call" | custom-call | tf_op jit(solution)/shard_map/give_back/pallas_call | solution.py:390
  306.3 2.3 copy.20

commit v4 on v3

--- a/solution.py
+++ b/solution.py
@@ -31,11 +31,16 @@
         return z, {"seq": self.seq, "exp": z * self.width + self.x}
 
     def in_plane(self, k):
-        j = lax.rem(self.me + k, self.plane)
-        return j, {
-            "seq": lax.div(j, self.width),
-            "exp": self.z * self.width + lax.rem(j, self.width),
-        }
+        core, chip = lax.rem(self.seq, 2), lax.div(self.seq, 2)
+        chips = self.plane // self.width // 2
+        steps = [(b, c, a) for a in range(2) for b in range(self.width) for c in range(chips)]
+        near = [step for step in steps if step[0] == 0 and step[1] == 0]
+        far = [step for step in steps if step[0] or step[1]]
+        far.sort(key=lambda step: (step[2], step[0] > 0 and step[1] > 0))
+        dx, dy, dc = (near[:1] + far + near[1:])[k]
+        seq = 2 * lax.rem(chip + dy, chips) + lax.rem(core + dc, 2)
+        x = lax.rem(self.x + dx, self.width)
+        return seq * self.width + x, {"seq": seq, "exp": self.z * self.width + x}
 
     def greet(self):
         barrier = pltpu.get_barrier_semaphore()
@@ -88,15 +93,10 @@
 
     lax.fori_loop(0, chunks, start_weights, 0)
     own = span(at.z, tokens, tokens)
-    ids[own, :] = ids_ref[...]
-    for c in range(chunks):
-        lines[c, own, :] = normed_ref[:, c * cw : (c + 1) * cw]
-    gate_sum[...] = jnp.zeros_like(gate_sum)
-    up_sum[...] = jnp.zeros_like(up_sum)
-    logits[...] = jnp.zeros_like(logits)
     at.greet()
+    ids[at.z] = ids_ref[...]
     for k in range(1, line):
-        remote(ids.at[own], ids.at[own], ids_send, ids_recv, at.on_line(k)[1]).start()
+        remote(ids.at[at.z], ids.at[at.z], ids_send, ids_recv, at.on_line(k)[1]).start()
 
     def line_start(c):
         for k in range(1, line):
@@ -135,8 +135,9 @@
                 plane_send.at[c], plane_recv.at[c], target,
             ).start()
         rows_in[c, mine, :] = pack[slot, mine, :]
-        logits[...] += jnp.dot(
-            lines[c], router_ref[span(c, cw, cw), :], preferred_element_type=jnp.float32
+        logits[...] += lax.dot_general(
+            router_ref[:, span(c, cw, cw)], lines[c], (((1,), (1,)), ((), ())),
+            preferred_element_type=jnp.float32,
         )
 
     def multiply(c):
@@ -149,32 +150,40 @@
             gate_sum[part, :] += jnp.dot(rows, gate[c], preferred_element_type=jnp.float32)
             up_sum[part, :] += jnp.dot(rows, up[c], preferred_element_type=jnp.float32)
 
-    def named(experts):
-        hits = jnp.zeros((ids.shape[0], experts.shape[1]), jnp.float32)
-        for k in range(TOP):
-            hits += jnp.where(ids[:, k : k + 1] == experts, 1.0, 0.0)
-        return hits
-
     def iota(shape, axis):
         return lax.broadcasted_iota(jnp.int32, shape, axis)
 
-    line_start(0)
-    line_start(1)
-    group = ids.shape[0]
-    ids_part = ids.at[pl.ds(0, (line - 1) * tokens)]
+    def named(experts):
+        blocks = []
+        for z in range(line):
+            hits = jnp.zeros((experts.shape[0], tokens), jnp.float32)
+            for k in range(TOP):
+                hits += jnp.where(ids[z, k : k + 1, :] == experts, 1.0, 0.0)
+            blocks.append(hits)
+        return jnp.concatenate(blocks, axis=1)
+
+    for c in range(chunks):
+        lines[c, own, :] = normed_ref[:, c * cw : (c + 1) * cw]
+        if c < 2:
+            line_start(c)
+    group = line * tokens
+    ids_part = ids.at[pl.ds(0, line - 1)]
     ids_bulk = remote(ids_part, ids_part, ids_send, ids_recv, at.on_line(1)[1])
     ids_bulk.wait_recv()
     experts_here = homes_ref[...] + at.z * width
     hits = named(experts_here)
-    before = jnp.where(iota((group, group), 1) < iota((group, group), 0), 1.0, 0.0)
+    before = jnp.where(iota((group, group), 0) < iota((group, group), 1), 1.0, 0.0)
     rank = jnp.dot(
-        before.astype(jnp.bfloat16), hits.astype(jnp.bfloat16), preferred_element_type=jnp.float32
-    )
-    place = jnp.where(hits > 0.0, rank, -1.0).T
+        hits.astype(jnp.bfloat16), before.astype(jnp.bfloat16), preferred_element_type=jnp.float32
+    )
+    place = jnp.where(hits > 0.0, rank, -1.0)
     seats = iota((cap, group), 0).astype(jnp.float32)
     for j in range(plane):
         seated = jnp.where(place[j : j + 1, :] == seats, 1.0, 0.0)
         pick[j * cap : (j + 1) * cap, :] = seated.astype(jnp.bfloat16)
+    logits[...] = jnp.zeros_like(logits)
+    gate_sum[...] = jnp.zeros_like(gate_sum)
+    up_sum[...] = jnp.zeros_like(up_sum)
 
     def step(c, carry):
         @pl.when(c + 2 < chunks)
@@ -191,15 +200,15 @@
         return carry
 
     lax.fori_loop(0, chunks, step, 0)
-    experts = logits.shape[1]
-    masked = jnp.where(named(iota((1, experts), 1)) > 0.0, logits[...], -jnp.inf)
-    raised = jnp.exp(masked - jnp.max(masked, axis=1, keepdims=True))
-    weights = raised / jnp.sum(raised, axis=1, keepdims=True)
-    select = jnp.where(iota((experts, experts_here.shape[1]), 0) == experts_here, 1.0, 0.0)
+    experts = logits.shape[0]
+    masked = jnp.where(named(iota((experts, 1), 0)) > 0.0, logits[...], -jnp.inf)
+    raised = jnp.exp(masked - jnp.max(masked, axis=0, keepdims=True))
+    weights = raised / jnp.sum(raised, axis=0, keepdims=True)
+    select = jnp.where(iota((experts_here.shape[0], experts), 1) == experts_here, 1.0, 0.0)
     weights_here = jnp.dot(
-        weights.astype(jnp.bfloat16), select.astype(jnp.bfloat16),
+        select.astype(jnp.bfloat16), weights.astype(jnp.bfloat16),
         preferred_element_type=jnp.float32,
-    ).T
+    )
     for j in range(plane):
         seat = pick[j * cap : (j + 1) * cap, :].astype(jnp.float32)
         mix_turned[j * cap : (j + 1) * cap, :] = weights_here[j : j + 1, :] * seat
@@ -354,8 +363,8 @@
     cw = width_d // chunks
     bf16, f32 = jnp.bfloat16, jnp.float32
 
-    homes = np.full((1, 128), -experts, np.int32)
-    homes[0, :plane] = [j // width * exp_count + j % width for j in range(plane)]
+    homes = np.full((128, 1), -experts, np.int32)
+    homes[:plane, 0] = [j // width * exp_count + j % width for j in range(plane)]
 
     vmem = pl.BlockSpec(memory_space=pltpu.VMEM)
     hbm = pl.BlockSpec(memory_space=pl.ANY)
@@ -369,10 +378,10 @@
         in_specs=[vmem, vmem, vmem, vmem, hbm, hbm],
         out_specs=(vmem, vmem),
         scratch_shapes=[
-            pltpu.VMEM((group, TOP), jnp.int32),
+            pltpu.VMEM((line, TOP, tokens), jnp.int32),
             pltpu.VMEM((total, group), bf16),
             pltpu.VMEM((total, group), f32),
-            pltpu.VMEM((group, experts), f32),
+            pltpu.VMEM((experts, group), f32),
             pltpu.VMEM((chunks, group, cw), bf16),
             pltpu.VMEM((2, total, cw), bf16),
             pltpu.VMEM((chunks, total, cw), bf16),
@@ -385,7 +394,7 @@
         ],
         compiler_params=kernel_params(0),
         name="dispatch",
-    )(normed, chosen_ids, jnp.asarray(homes), router_weight, w_gate, w_up)
+    )(normed, chosen_ids.T, jnp.asarray(homes), router_weight.T, w_gate, w_up)
 
     return pl.pallas_call(
         functools.partial(return_kernel, line, width, seq_count, cap),
@@ -495,25 +504,49 @@
             part, part, query_send.at[h], query_recv.at[h], {"seq": lax.rem(me + 1, seq_count)}
         )
 
-    def attend_head(h, carry):
+    def attend_block(h, b):
+        rows = slice(b * tokens, (b + 1) * tokens)
+        reach = prefix_total + (b + 1) * tokens
+        scores = lax.dot_general(
+            query[h, rows, :], key[:reach, :], (((1,), (1,)), ((), ())),
+            preferred_element_type=f32,
+        ) * HEAD_SIZE ** (-0.5) + mask[rows, :reach]
+        raised = jnp.exp(scores - jnp.max(scores, axis=1, keepdims=True))
+        mixed = jnp.dot(raised.astype(bf16), value[:reach, :], preferred_element_type=f32)
+        mixed = mixed / jnp.sum(raised, axis=1, keepdims=True)
+        attended[rows, span(h, HEAD_SIZE, HEAD_SIZE)] = mixed.astype(bf16)
+
+    def far_head(h, carry):
         query_bulk(h).wait_recv()
-        for b in range(seq_count):
-            rows = slice(b * tokens, (b + 1) * tokens)
-            reach = prefix_total + (b + 1) * tokens
-            scores = lax.dot_general(
-                query[h, rows, :], key[:reach, :], (((1,), (1,)), ((), ())),
-                preferred_element_type=f32,
-            ) * HEAD_SIZE ** (-0.5) + mask[rows, :reach]
-            raised = jnp.exp(scores - jnp.max(scores, axis=1, keepdims=True))
-            mixed = jnp.dot(raised.astype(bf16), value[:reach, :], preferred_element_type=f32)
-            mixed = mixed / jnp.sum(raised, axis=1, keepdims=True)
-            attended[rows, span(h, HEAD_SIZE, HEAD_SIZE)] = mixed.astype(bf16)
-        return carry
-
-    lax.fori_loop(0, heads, attend_head, 0)
+        for y in range(chips):
+
+            @pl.when(chip != y)
+            def _():
+                attend_block(h, 2 * y)
+                attend_block(h, 2 * y + 1)
+
+        return carry
+
+    def near_head(h, carry):
+        for y in range(chips):
+
+            @pl.when(chip == y)
+            def _():
+                attend_block(h, 2 * y)
+                attend_block(h, 2 * y + 1)
+
+        return carry
 
     def pair_bulk(c):
-        return remote(pair_out.at[c], pair_in.at[c], pair_send.at[c], pair_recv.at[c], partner)
+        return remote(
+            pair_out.at[c, pl.ds(1, chips - 1)], pair_in.at[c, pl.ds(1, chips - 1)],
+            pair_send.at[0, c], pair_recv.at[0, c], partner,
+        )
+
+    def near_bulk(c):
+        return remote(
+            pair_out.at[c, 0], pair_in.at[c, 0], pair_send.at[1, c], pair_recv.at[1, c], partner
+        )
 
     def far_bulk(c):
         return remote(far_out.at[c], far_in.at[c], far_send.at[c], far_recv.at[c], partner)
@@ -524,28 +557,24 @@
 
     def pair_step(c):
         weight_copy(c).wait()
-        for k in range(chips):
+        for k in range(1, chips):
             there = lax.rem(chip + k, chips)
             pair_out[c, k] = project(c, 2 * there + 1 - core).astype(bf16)
         pair_bulk(c).start()
-        for k in range(chips):
+        for k in range(1, chips):
             there = lax.rem(chip + k, chips)
-            own_sum[lax.rem(c, 2), k] = project(c, 2 * there + core)
+            own_sum[lax.rem(c, 2), k - 1] = project(c, 2 * there + core)
 
     def far_step(c):
         pair_bulk(c).wait_recv()
         for k in range(1, chips):
             there = lax.rem(chip + k, chips)
-            both = own_sum[lax.rem(c, 2), k] + pair_in[c, k].astype(f32)
+            both = own_sum[lax.rem(c, 2), k - 1] + pair_in[c, k].astype(f32)
             far_out[c, k - 1] = both.astype(bf16)
             remote(
                 far_out.at[c, k - 1], far_in.at[c, k - 1], far_send.at[c], far_recv.at[c],
                 {"seq": 2 * there + core},
             ).start()
-        columns = span(c, cw, cw)
-        hidden_ref[:, columns] = (
-            resid_ref[:, columns].astype(f32) + own_sum[lax.rem(c, 2), 0] + pair_in[c, 0].astype(f32)
-        )
 
     def step(c, carry):
         @pl.when(c < chunks)
@@ -558,12 +587,23 @@
 
         return carry
 
+    def near_step(c, carry):
+        pair_out[c, 0] = project(c, 2 * chip + 1 - core).astype(bf16)
+        near_bulk(c).start()
+        columns = span(c, cw, cw)
+        hidden_ref[:, columns] = resid_ref[:, columns].astype(f32) + project(c, me)
+        return carry
+
+    lax.fori_loop(0, heads, far_head, 0)
     lax.fori_loop(0, chunks + 1, step, 0)
+    lax.fori_loop(0, heads, near_head, 0)
+    lax.fori_loop(0, chunks, near_step, 0)
 
     def sum_step(c, square):
+        near_bulk(c).wait_recv()
         far_bulk(c).wait_recv()
         columns = span(c, cw, cw)
-        total = hidden_ref[:, columns]
+        total = hidden_ref[:, columns] + pair_in[c, 0].astype(f32)
         for k in range(chips - 1):
             total += far_in[c, k].astype(f32)
         hidden_ref[:, columns] = total
@@ -584,6 +624,7 @@
 
     def drain(c, carry):
         pair_bulk(c).wait_send()
+        near_bulk(c).wait_send()
         far_bulk(c).wait_send()
         return carry
 
@@ -640,11 +681,11 @@
             pltpu.VMEM((chunks, heads * HEAD_SIZE, cw), bf16),
             pltpu.VMEM((chunks, chips, tokens, cw), bf16),
             pltpu.VMEM((chunks, chips, tokens, cw), bf16),
-            pltpu.VMEM((2, chips, tokens, cw), f32),
+            pltpu.VMEM((2, chips - 1, tokens, cw), f32),
             pltpu.VMEM((chunks, chips - 1, tokens, cw), bf16),
             pltpu.VMEM((chunks, chips - 1, tokens, cw), bf16),
             dma, dma, dma, dma, dma((heads,)), dma((heads,)),
-            dma((chunks,)), dma((chunks,)), dma((chunks,)), dma((chunks,)), dma((chunks,)),
+            dma((2, chunks)), dma((2, chunks)), dma((chunks,)), dma((chunks,)), dma((chunks,)),
         ],
         compiler_params=kernel_params(2),
         name="attend",

time: 309 us -> 297 us (0.961)
  Pallas kernels: 301 us -> 293 us
  local copies, waits for them, and re-layouts: 5.95 us -> 2.29 us
    pallas_call x1, Pallas kernels: 127 us -> 121 us  [experts_layer(): pl.pallas_call(functools.partial(dispatch_kernel, line, width, seq_count,...]
    unnamed x3 -> x1, local copies, waits for them, and re-layouts: 5.95 us -> 2.29 us
where the time goes in v4:
time: 297 us
  Pallas kernels  293 us (99%)
    pallas_call x1, Pallas kernels, experts_layer(): pl.pallas_call(functools.partial(return_kernel, line, width, seq_count, c...  121 us
    pallas_call x1, Pallas kernels, experts_layer(): pl.pallas_call(functools.partial(dispatch_kernel, line, width, seq_count,...  121 us
    pallas_call x1, Pallas kernels, per_device(): pl.pallas_call(functools.partial(attend_kernel, heads, group_length, pref...  51.3 us

profile of v4, /device:TPU:0, one launch (start us, length us, event | category | flops | bytes accessed | tf_op | source)
XLA Modules:
  0.0 296.8 jit_solution(14259930911093222825)
XLA Ops:
  0.7 0.6 compare_select_fusion.bias_ref
  1.2 51.3 %attend.1 = (f32[128,4096]{1,0:T(8,128)}, bf16[128,4096]{1,0:T(8,128)(2,1)}) custom-call(bf16[128,4096]{1,0:T(8,128)(2,1)} %bitcast.21, bf16[128,512]{1,0:T(8,128)(2,1)} %bitcast.24, bf16[128,512]{1,0:T(8,128)(2,1)} %bitcast.25, bf16[4,64,128]{2,1,0:T(8,128)(2,1)} %bitcast.26, bf16[4,64,128]{2,1,0:T(8,128)(2,1)} %bitcast.27, ...), custom_call_target="tpu_custom_call" | custom-call | tf_op jit(solution)/shard_map/attend/pallas_call | solution.py:667
  52.5 120.6 %dispatch.1 = (bf16[1152,768]{1,0:T(8,128)(2,1)}, bf16[512,1152]{1,0:T(8,128)(2,1)}) custom-call(bf16[128,4096]{1,0:T(8,128)(2,1)} %get-tuple-element.9.normed_ref, s32[8,128]{1,0:T(8,128)} %bitcast.29, s32[128,1]{1,0:T(8,128)} %constant.6.clone.homes_ref, bf16[32,4096]{1,0:T(8,128)(2,1)} %bitcast.23, bf16[4096,768]{1,0:T(8,128)(2,1)} %bitcast.17, ...), custom_call_target="tpu_custom_call" | custom-call | tf_op jit(solution)/shard_map/dispatch/pallas_call | solution.py:372
  173.1 121.4 %give_back.1 = bf16[128,4096]{1,0:T(8,128)(2,1)} custom-call(bf16[1152,768]{1,0:T(8,128)(2,1)} %get-tuple-element.10.act_ref, bf16[512,1152]{1,0:T(8,128)(2,1)} %get-tuple-element.11.mix_ref, f32[128,4096]{1,0:T(8,128)} %get-tuple-element.12.hidden_ref, bf16[768,4096]{1,0:T(8,128)(2,1)} %bitcast.19), custom_call_target="tpu_custom_call" | custom-call | tf_op jit(solution)/shard_map/give_back/pallas_call | solution.py:399
  294.5 2.3 copy.18
